TPU v7x, 256 devices: a whole 4x4x8 slice. The times are simulated.
256 devices in a mesh: blk: 32 (over y_lo, z, core), tensor: 8 (over x, y_hi).
Axes of the slice: x: 4, y: 4 (y_hi: 2, y_lo: 2; y = y_hi * 2 + y_lo), z: 8, core: 2. Of those that a mesh axis runs over, the one named last changes fastest.
Arguments:
- a_query: bfloat16 [16384, 2048], P('blk', 'tensor'), may hold values from -24 to 24
- a_key: bfloat16 [16384, 128], P(('blk', 'tensor')), may hold values from -4 to 4
- a_value: bfloat16 [16384, 128], P(('blk', 'tensor')), may hold values from -6 to 6
- b_query: bfloat16 [1536, 2048], P('blk', 'tensor'), may hold values from -24 to 24
- b_key: bfloat16 [1536, 128], P('blk'), may hold values from -4 to 4
- b_value: bfloat16 [1536, 128], P('blk'), may hold values from -6 to 6
- cache_key: bfloat16 [65536, 128], P(('blk', 'tensor')), may hold values from -4 to 4
- cache_value: bfloat16 [65536, 128], P(('blk', 'tensor')), may hold values from -6 to 6
- a_positions: int32 [16384], replicated, may hold values from 0 to 16383, as said below
- cache_lengths: int32 [32], replicated, may hold values from 1 to 2048, 61440 in all
Outputs:
- a_output: bfloat16 [16384, 2048], P('blk', 'tensor')
- b_output: bfloat16 [1536, 2048], P('blk', 'tensor')
Inputs may be any that keep to these rules, and one draw needn't show every extreme that they name: `a_positions`: a permutation of 0 to 16383 made of blocks of 256 consecutive positions in increasing order; the rows of one index of blk hold two blocks, numbers c and 63 - c for some c, in either order.
All inputs are finite; a program needn't handle non-finite values.
Results may differ from a plain program's by a relative error of at most 0.012.
Values may be sent and summed in bfloat16 or wider, within the bound.
A program may use at most 64 MiB of HBM per device.

v0:
```python
import math

import jax
import jax.numpy as jnp
from jax import lax
from jax.sharding import PartitionSpec as P

LOWEST = -1e30


def attend(carry, query, query_pos, keys, values, key_pos):
    largest, total, accum = carry
    scores = jnp.einsum(
        "rhd,kd->hrk", query, keys, preferred_element_type=jnp.float32
    ) * query.shape[2] ** (-0.5)
    visible = (key_pos[None, :] <= query_pos[:, None])[None]
    scores = jnp.where(visible, scores, LOWEST)
    new_largest = jnp.maximum(largest, jnp.max(scores, axis=2))
    weights = jnp.where(visible, jnp.exp(scores - new_largest[:, :, None]), 0.0)
    factor = jnp.exp(largest - new_largest)
    total = total * factor + jnp.sum(weights, axis=2)
    accum = accum * factor[:, :, None] + jnp.einsum(
        "hrk,kd->hrd", weights.astype(jnp.bfloat16), values, preferred_element_type=jnp.float32
    )
    return (new_largest, total, accum)


def over_blocks(carry, keys, values, key_pos, span, advance):
    count = keys.shape[0] // span

    def one_block(state, item):
        return (advance(state, item[0], item[1], item[2]), None)

    carry, unused = lax.scan(
        one_block,
        carry,
        (
            keys.reshape(count, span, keys.shape[1]),
            values.reshape(count, span, values.shape[1]),
            key_pos.reshape(count, span),
        ),
    )
    return carry


def shards(
    a_query,
    a_key,
    a_value,
    b_query,
    b_key,
    b_value,
    cache_key,
    cache_value,
    a_positions,
    cache_lengths,
):
    width = a_key.shape[1]
    head_count = a_query.shape[1] // width
    a_rows = a_query.shape[0]
    group = lax.axis_index("blk")

    def start_state(count):
        return (
            jnp.full((head_count, count), LOWEST, jnp.float32),
            jnp.zeros((head_count, count), jnp.float32),
            jnp.zeros((head_count, count, width), jnp.float32),
        )

    query_pos = lax.dynamic_slice_in_dim(a_positions, group * a_rows, a_rows)
    queries = a_query.reshape(a_rows, head_count, width)
    sections = 2
    span_limit = a_rows // 2
    section_rows = a_rows // sections
    section_queries = [
        queries[member * section_rows : (member + 1) * section_rows] for member in range(sections)
    ]
    section_pos = [
        query_pos[member * section_rows : (member + 1) * section_rows] for member in range(sections)
    ]

    def advance_a(states, keys, values, key_pos):
        result = []
        for member in range(sections):

            def compute(state, member=member):
                return attend(
                    state, section_queries[member], section_pos[member], keys, values, key_pos
                )

            result.append(
                lax.cond(
                    jnp.min(key_pos) <= jnp.max(section_pos[member]),
                    compute,
                    lambda state: state,
                    states[member],
                )
            )
        return tuple(result)

    initial = tuple((start_state(section_rows) for member in range(sections)))
    group_keys, group_values = (
        lax.all_gather(a_key, "tensor", axis=0, tiled=True),
        lax.all_gather(a_value, "tensor", axis=0, tiled=True),
    )
    pieces = (
        lax.all_gather(group_keys, "blk", axis=0, tiled=True),
        lax.all_gather(group_values, "blk", axis=0, tiled=True),
    )
    count = pieces[0].shape[0]
    key_pos = a_positions
    states = over_blocks(
        initial, pieces[0], pieces[1], key_pos, math.gcd(count, span_limit), advance_a
    )
    outputs = []
    for member in range(sections):
        largest, total, accum = states[member]
        outputs.append(accum / total[:, :, None])
    a_output = (
        jnp.concatenate(outputs, axis=1)
        .transpose(1, 0, 2)
        .reshape(a_rows, head_count * width)
        .astype(jnp.bfloat16)
    )
    all_queries = lax.all_gather(b_query, "blk", axis=0, tiled=True)
    b_rows = all_queries.shape[0]
    b_count = b_query.shape[0]
    b_heads = all_queries.reshape(b_rows, head_count, width)
    every_pos = jnp.arange(b_rows, dtype=jnp.int32)
    limit = lax.dynamic_index_in_dim(cache_lengths, group, 0, keepdims=False)

    def advance_b(state, keys, values, key_pos):
        return attend(state, b_heads, every_pos, keys, values, key_pos)

    pieces = (
        lax.all_gather(cache_key, "tensor", axis=0, tiled=True),
        lax.all_gather(cache_value, "tensor", axis=0, tiled=True),
    )
    count = pieces[0].shape[0]
    slots = jnp.arange(count, dtype=jnp.int32)
    key_pos = jnp.where(slots < limit, -1, b_rows).astype(jnp.int32)
    state = over_blocks(
        start_state(b_rows), pieces[0], pieces[1], key_pos, math.gcd(count, 512), advance_b
    )
    new_pos = group * b_count + jnp.arange(b_count, dtype=jnp.int32)
    largest, total, accum = attend(state, b_heads, every_pos, b_key, b_value, new_pos)
    partial_out = (accum / total[:, :, None]).astype(jnp.bfloat16)
    best = lax.pmax(largest, "blk")
    share = total * jnp.exp(largest - best)
    numer, denom = (
        lax.psum_scatter(
            partial_out.astype(jnp.float32) * share[:, :, None],
            "blk",
            scatter_dimension=1,
            tiled=True,
        ),
        lax.psum_scatter(share, "blk", scatter_dimension=1, tiled=True),
    )
    merged = numer / denom[:, :, None]
    b_output = merged.transpose(1, 0, 2).reshape(b_count, head_count * width).astype(jnp.bfloat16)
    return (a_output, b_output)


def solution(mesh):
    in_specs = (
        P("blk", "tensor"),
        P(("blk", "tensor"), None),
        P(("blk", "tensor"), None),
        P("blk", "tensor"),
        P("blk", None),
        P("blk", None),
        P(("blk", "tensor"), None),
        P(("blk", "tensor"), None),
        P(),
        P(),
    )
    out_specs = (P("blk", "tensor"), P("blk", "tensor"))
    return jax.shard_map(shards, mesh=mesh, in_specs=in_specs, out_specs=out_specs, check_vma=False)
```

profile of v0, /device:TPU:33, one launch (start us, length us, event | category | flops | bytes accessed | tf_op | source)
XLA Modules:
  0.0 958.5 jit_solution(16622800322509500663)
XLA Ops:
  7.3 1.3 dynamic_slice.35
  9.3 37.1 %all_gather.26 = bf16[1536,256]{1,0:T(8,128)(2,1)S(1)} all-gather(bf16[48,256]{1,0:T(8,128)(2,1)} %param.21), channel_id=1, replica_groups=mesh['blk'=32,'tensor'=8] {'blk'}, dimensions={0}, use_global_device_ids=true | all-gather | bytes 811008 | tf_op jit(solution)/shard_map/all_gather | solution.py:125
  47.0 29.3 %all_gather.25 = bf16[2048,128]{1,0:T(8,128)(2,1)S(1)} all-gather(bf16[256,128]{1,0:T(8,128)(2,1)} %param.24), channel_id=1, replica_groups=mesh['blk'=32,'tensor'=8] {'tensor'}, dimensions={0}, use_global_device_ids=true | all-gather | bytes 589824 | tf_op jit(solution)/shard_map/all_gather | solution.py:136
  76.3 29.2 %all_gather.27 = bf16[2048,128]{1,0:T(8,128)(2,1)S(1)} all-gather(bf16[256,128]{1,0:T(8,128)(2,1)S(1)} %copy-done.4), channel_id=1, replica_groups=mesh['blk'=32,'tensor'=8] {'tensor'}, dimensions={0}, use_global_device_ids=true | all-gather | bytes 589824 | tf_op jit(solution)/shard_map/all_gather | solution.py:137
  105.5 54.2 %while.37 = (s32[]{:T(128)}, f32[2,1536]{1,0:T(2,128)S(1)}, f32[2,1536]{1,0:T(2,128)S(1)}, f32[2,1536,128]{2,1,0:T(8,128)}, s32[4,512]{1,0:T(4,128)S(1)}, /*inde...) while((s32[]{:T(128)}, f32[2,1536]{1,0:T(2,128)S(1)}, ...), condition=%wide.region_16.17_spmd.clone, body=%wide.region_13.16_spmd.clone.sunk | while | flops 827735040 | bytes 51583128 | solution.py:34
  106.0 4.1 fusion.85
  110.1 4.6 fusion.87
  114.8 3.4 fusion.89
  118.8 4.1 fusion.85
  122.9 4.6 fusion.87
  127.5 4.5 fusion.89
  132.6 4.1 fusion.85
  136.7 4.6 fusion.87
  141.4 4.5 fusion.89
  146.4 4.1 fusion.85
  150.5 4.6 fusion.87
  155.2 4.5 fusion.89
  160.1 110.6 %pmax.7 = f32[2,1536]{1,0:T(2,128)S(1)} all-reduce(f32[2,1536]{1,0:T(2,128)S(1)} %max.14), channel_id=1, replica_groups=mesh['blk'=32,'tensor'=8] {'blk'}, use_global_device_ids=true, to_apply=%region_19.20 | all-reduce | flops 3072 | bytes 24576 | tf_op jit(solution)/shard_map/pmax | solution.py:148
  270.9 1.2 copy.44
  272.3 4.3 fusion.48
  276.7 30.0 %all_gather.23 = bf16[512,128]{1,0:T(8,128)(2,1)} all-gather(bf16[64,128]{1,0:T(8,128)(2,1)S(1)} %copy-done.5), channel_id=1, replica_groups=mesh['blk'=32,'tensor'=8] {'tensor'}, dimensions={0}, use_global_device_ids=true | all-gather | bytes 147456 | tf_op jit(solution)/shard_map/all_gather | solution.py:104
  306.8 30.1 %all_gather.21 = bf16[512,128]{1,0:T(8,128)(2,1)} all-gather(bf16[64,128]{1,0:T(8,128)(2,1)S(1)} %copy-done.6), channel_id=1, replica_groups=mesh['blk'=32,'tensor'=8] {'tensor'}, dimensions={0}, use_global_device_ids=true | all-gather | bytes 147456 | tf_op jit(solution)/shard_map/all_gather | solution.py:103
  338.1 48.0 %reduce-scatter.7.cloned.1.call-done = f32[48,2]{1,0:T(8,128)} async-done(((f32[1536,2]{1,0:T(8,128)}), f32[48,2]{1,0:T(8,128)}) %reduce-scatter.7.cloned.1.call-update) | async-done | bytes 400
  386.9 115.4 %reduce-scatter.5.cloned.1.call-done = f32[2,48,128]{2,1,0:T(8,128)} async-done(((f32[2,1536,128]{2,1,0:T(8,128)}), f32[2,48,128]{2,1,0:T(8,128)}) %reduce-scatter.5.cloned.1.call-update) | async-done | bytes 49168 | tf_op jit(solution)/shard_map/reduce_scatter | solution.py:151
  502.4 1.5 copy_bitcast_fusion.1
  503.9 70.3 %all-gather.5.cloned.1.call-done = bf16[16384,128]{1,0:T(8,128)(2,1)} async-done(((bf16[512,128]{1,0:T(8,128)(2,1)}), bf16[16384,128]{1,0:T(8,128)(2,1)}) %all-gather.5.cloned.1.call-update) | async-done | bytes 4194320 | tf_op jit(solution)/shard_map/all_gather | solution.py:108
  574.2 68.2 %all-gather.3.cloned.1.call-done = bf16[16384,128]{1,0:T(8,128)(2,1)} async-done(((bf16[512,128]{1,0:T(8,128)(2,1)}), bf16[16384,128]{1,0:T(8,128)(2,1)}) %all-gather.3.cloned.1.call-update) | async-done | bytes 4194320 | tf_op jit(solution)/shard_map/all_gather | solution.py:107
  642.5 308.6 %while.36 = (s32[]{:T(128)}, f32[2,256]{1,0:T(2,128)S(1)}, f32[2,256]{1,0:T(2,128)S(1)}, f32[2,256,128]{2,1,0:T(8,128)S(1)}, f32[2,256]{1,0:T(2,128)S(1)}, /*ind...) while((s32[]{:T(128)}, f32[2,256]{1,0:T(2,128)S(1)}, ...), condition=%wide.region_12.13_spmd, body=%wide.region_2.12_spmd.sunk | while | flops 136972544 | bytes 5577141 | solution.py:34
  645.2 0.9 conditional.5
  650.0 0.9 conditional.5
  654.8 0.9 conditional.5
  659.6 0.9 conditional.5
  684.6 0.9 conditional.5
  689.4 0.9 conditional.5
  698.1 0.9 conditional.5
  708.6 0.9 conditional.5
  713.4 0.9 conditional.5
  723.0 0.9 conditional.5
  732.6 0.9 conditional.5
  737.5 0.9 conditional.5
  742.3 0.9 conditional.5
  747.1 0.9 conditional.5
  751.9 0.9 conditional.5
  756.7 0.9 conditional.5
  785.5 0.9 conditional.5
  790.3 0.9 conditional.5
  795.1 0.9 conditional.5
  804.8 0.9 conditional.5
  813.5 0.9 conditional.5
  824.0 0.9 conditional.5
  843.2 0.9 conditional.5
  848.0 0.9 conditional.5
  852.8 0.9 conditional.5
  857.6 0.9 conditional.5
  862.4 0.9 conditional.5
  867.3 0.9 conditional.5
  872.1 0.9 conditional.5
  880.8 0.9 conditional.5
  900.9 0.9 conditional.5
  905.7 0.9 conditional.5
  915.3 0.9 conditional.5
  929.7 0.9 conditional.5
  938.4 0.9 conditional.5
  949.0 0.9 conditional.5
  (754 shorter events, 187.5 us)
Async XLA Ops:
  7.2 265.0 %copy-start = (bf16[48,128]{1,0:T(8,128)(2,1)S(1)}, bf16[48,128]{1,0:T(8,128)(2,1)}, u32[]{:S(2)}) copy-start(bf16[48,128]{1,0:T(8,128)(2,1)} %param.23) | copy-start | bytes 36868
  7.2 69.2 %copy-start.4 = (bf16[256,128]{1,0:T(8,128)(2,1)S(1)}, bf16[256,128]{1,0:T(8,128)(2,1)}, u32[]{:S(2)}) copy-start(bf16[256,128]{1,0:T(8,128)(2,1)} %param.25) | copy-start | bytes 196612
  7.2 378.9 %reduce-scatter.7.cloned.1.call-start = ((), (), s32[]{:S(2)}) async-start(), calls=%async_computation.5 | async-start | bytes 811008
  105.5 54.3 %copy-start.7 = (bf16[48,128]{1,0:T(8,128)(2,1)S(1)}, bf16[48,128]{1,0:T(8,128)(2,1)}, u32[]{:S(2)}) copy-start(bf16[48,128]{1,0:T(8,128)(2,1)} %param.22) | copy-start | bytes 36868
  110.1 4.7 copy-start.1
  122.9 4.7 copy-start.1
  136.7 4.7 copy-start.1
  150.5 4.7 copy-start.1
  272.2 230.2 %reduce-scatter.5.cloned.1.call-start = ((), (), s32[]{:S(2)}) async-start(), calls=%async_computation.4 | async-start | bytes 1622016 | tf_op jit(solution)/shard_map/reduce_scatter | solution.py:151
  272.2 4.4 copy-start.5
  272.2 34.5 %copy-start.6 = (bf16[64,128]{1,0:T(8,128)(2,1)S(1)}, bf16[64,128]{1,0:T(8,128)(2,1)}, u32[]{:S(2)}) copy-start(bf16[64,128]{1,0:T(8,128)(2,1)} %param.19) | copy-start | bytes 49156
  272.2 64.6 %copy-start.3 = (s32[16384]{0:T(1024)S(1)}, s32[16384]{0:T(1024)}, u32[]{:S(2)}) copy-start(s32[16384]{0:T(1024)} %param.26) | copy-start | bytes 196612
  272.2 64.7 %copy-start.2 = (bf16[512,256]{1,0:T(8,128)(2,1)S(1)}, bf16[512,256]{1,0:T(8,128)(2,1)}, u32[]{:S(2)}) copy-start(bf16[512,256]{1,0:T(8,128)(2,1)} %param.18) | copy-start | bytes 786436
  276.6 297.6 %all-gather.5.cloned.1.call-start = ((), (), s32[]{:S(2)}) async-start(), calls=%async_computation.3 | async-start | bytes 4325376 | tf_op jit(solution)/shard_map/all_gather | solution.py:108
  306.7 335.7 %all-gather.3.cloned.1.call-start = ((), (), s32[]{:S(2)}) async-start(), calls=%async_computation.2 | async-start | bytes 4325376 | tf_op jit(solution)/shard_map/all_gather | solution.py:107
Sparse Core Ops, SparseCore 0:
  272.3 113.8 reduce-scatter.6
  388.8 113.5 reduce-scatter.4
  504.2 69.8 all-gather.4
  575.9 66.4 all-gather.2
where the time goes:
time: 966 us; the launch traced here: 959 us
  waiting for transfers between devices  302 us (31%)
  blocking collectives  266 us (28%)
  loops' own time  156 us (16%)
  other arithmetic  80.3 us (8%)
  matrix products  78.2 us (8%)
  local copies, waits for them, and re-layouts  61.6 us (6%)
  between operations  14 us (1%)
    another operation x2, loops' own time, over_blocks(): lax.scan(one_block, carry, (keys.reshape(count, span, keys.shape[1]), val...  152 us
    reduce_scatter x1, waiting for transfers between devices, shards(): lax.psum_scatter(partial_out.astype(jnp.float32) * share[:, :, None], 'bl...  115 us
    pmax x1, blocking collectives, shards(): best = lax.pmax(largest, 'blk')  111 us
    all_gather x1, waiting for transfers between devices, shards(): lax.all_gather(group_values, 'blk', axis=0, tiled=True)  70.3 us
    all_gather x1, waiting for transfers between devices, shards(): lax.all_gather(group_keys, 'blk', axis=0, tiled=True)  68.2 us
    squeeze x64, local copies, waits for them, and re-layouts, over_blocks(): lax.scan(one_block, carry, (keys.reshape(count, span, keys.shape[1]), val...  56.7 us
    unnamed x5, waiting for transfers between devices  48.1 us
    dot_general x70, matrix products, attend(): jnp.einsum('hrk,kd->hrd', weights.astype(jnp.bfloat16), values, preferred...  45.4 us
  transfers between devices with their start and end apart: 4, of which 4 were waited for; matrix products, arithmetic and copies ran while one was open for 1% of the time, Pallas kernels for 0%

commit v1 on v0

v1 whole, which is shorter than its diff:
```python
import functools
import math

import jax
import jax.numpy as jnp
from jax import lax
from jax.experimental import pallas as pl
from jax.experimental.pallas import tpu as pltpu
from jax.sharding import PartitionSpec as P

HD = 128
BLOCK = 256
CHUNK = 4
OWNERS = 4
SCALE2 = HD ** (-0.5) * math.log2(math.e)
LOWEST = -1e30
NT = (((1,), (1,)), ((), ()))
NN = (((1,), (0,)), ((), ()))
MESH = pl.DeviceIdType.MESH


def dot(a, b, dims):
    return lax.dot_general(a, b, dims, preferred_element_type=jnp.float32)


class Copy:
    def __init__(self, book, view, device):
        self.book, self.view, self.device = book, view, device
        self.index = len(book.copies)
        book.copies.append(self)

    def make(self):
        return pltpu.make_async_remote_copy(
            src_ref=self.view(),
            dst_ref=self.view(),
            send_sem=self.book.send.at[self.index],
            recv_sem=self.book.recv.at[self.index],
            device_id=self.device,
            device_id_type=MESH,
        )


class Book:
    def __init__(self, send, recv):
        self.send, self.recv, self.copies = send, recv, []


class Gather:
    def __init__(self, book, views, order, axes, sibling):
        self.steps, self.forwards = [], []
        done = []
        for number, axis in enumerate(order):
            size, at, device = axes[axis]
            final = number == len(order) - 1 and sibling is not None
            if final:
                self.forwards = [[] for step in self.steps]
                self.forwards.append(
                    [Copy(book, v, sibling) for v in views(tuple(done), axis, at, None)]
                )
            for k in range(1, size // 2 + 1):
                sends, arrived = [], []
                for way in (1, -1):
                    if size == 2 and way == -1:
                        continue
                    half = None
                    if 2 * k == size and size > 2:
                        half = 0 if way == 1 else 1
                    out = (at - way * (k - 1) + 2 * size) % size
                    got = (at - way * k + 2 * size) % size
                    for v in views(tuple(done), axis, out, half):
                        sends.append(Copy(book, v, device(way)))
                    if final:
                        for v in views(tuple(done), axis, got, half):
                            arrived.append(Copy(book, v, sibling))
                self.steps.append(sends)
                if final:
                    self.forwards.append(arrived)
            done.append(axis)

    def run(self, step):
        if step > len(self.steps):
            return
        if step > 0:
            for copy in self.steps[step - 1]:
                copy.make().wait_recv()
        if step < len(self.steps):
            for copy in self.steps[step]:
                copy.make().start()
        if step < len(self.forwards):
            for copy in self.forwards[step]:
                copy.make().start()

    def siblings(self):
        for group in self.forwards:
            for copy in group:
                copy.make().wait_recv()


def sizes_of(blocks, heads):
    y_lo, y_hi = 2, 2
    return heads // y_hi, y_hi, y_lo, blocks // (2 * y_lo)


def exchange_kernel(
    blocks,
    heads,
    lengths,
    a_key,
    a_value,
    b_query,
    b_key,
    b_value,
    cache_key,
    cache_value,
    key_x,
    value_y,
    key_z,
    value_z,
    b_out,
    q_all,
    k_all,
    v_all,
    k_buf,
    v_buf,
    column,
    part,
    stat,
    part_in,
    stat_in,
    send,
    recv,
    merge_send,
    merge_recv,
    local,
):
    X, YH, YL, Z = sizes_of(blocks, heads)
    Y = YH * YL
    me, t = lax.axis_index("blk"), lax.axis_index("tensor")
    yl, z, c = me // (2 * Z), (me // 2) % Z, me % 2
    x, yh = t // YH, t % YH
    y = yh * YL + yl

    def dev(x, y, z, c):
        return ((y % YL) * (2 * Z) + z * 2 + c, x * YH + y // YL)

    axes = {
        "x": (X, x, lambda way: dev((x + way + X) % X, y, z, c)),
        "y": (Y, y, lambda way: dev(x, (y + way + Y) % Y, z, c)),
        "z": (Z, z, lambda way: dev(x, y, (z + way + Z) % Z, c)),
        "yl": (YL, yl, lambda way: dev(x, yh * YL + (1 - yl), z, c)),
        "yh": (YH, yh, lambda way: dev(x, (1 - yh) * YL + yl, z, c)),
    }
    sibling = dev(x, y, z, 1 - c)
    every = slice(None)

    def a_views(arrays, lone):
        def views(done, axis, at, half):
            chosen = arrays
            zs = every if "z" in done else (at if axis == "z" else z)
            if half is not None:
                if len(arrays) == 2:
                    chosen = arrays[half:half + 1]
                elif "z" in done:
                    zs = pl.ds(half * (Z // 2), Z // 2)
                elif half != lone:
                    chosen = []
            xs = every if "x" in done else (at if axis == "x" else x)
            if "y" in done:
                yls, yhs = every, every
            elif axis == "y":
                yls, yhs = at % YL, at // YL
            else:
                yls, yhs = yl, yh
            return [lambda a=a: a.at[yls, zs, c, xs, yhs] for a in chosen]

        return views

    def cache_views(done, axis, at, half):
        chosen = [k_all, v_all] if half is None else [k_all, v_all][half:half + 1]
        xs = at if axis == "x" else x
        yhs = every if "yh" in done else (at if axis == "yh" else yh)
        return [lambda a=a: a.at[xs, yhs] for a in chosen]

    def query_views(done, axis, at, half):
        if half == 1:
            return []
        yls = every if "yl" in done else (at if axis == "yl" else yl)
        zs = at if axis == "z" else z
        return [lambda: q_all.at[yls, zs, c]]

    book = Book(send, recv)
    caches = Gather(book, cache_views, ["yh", "x"], axes, None)
    asked = Gather(book, query_views, ["yl", "z"], axes, sibling)
    pieces = [
        Gather(book, a_views([key_x], 0), ["z", "y", "x"], axes, sibling),
        Gather(book, a_views([value_y], 1), ["z", "x", "y"], axes, sibling),
        Gather(book, a_views([key_z, value_z], 0), ["x", "y", "z"], axes, sibling),
    ]

    cut = key_x.shape[5]
    rows = a_key.shape[0]
    locals_ = [
        (cache_key, k_all.at[x, yh]),
        (cache_value, v_all.at[x, yh]),
        (b_query, q_all.at[yl, z, c]),
        (a_key.at[pl.ds(0, cut)], key_x.at[yl, z, c, x, yh]),
        (a_value.at[pl.ds(0, cut)], value_y.at[yl, z, c, x, yh]),
        (a_key.at[pl.ds(cut, rows - cut)], key_z.at[yl, z, c, x, yh]),
        (a_value.at[pl.ds(cut, rows - cut)], value_z.at[yl, z, c, x, yh]),
    ]
    locals_ = [
        pltpu.make_async_copy(a, b, local.at[i]) for i, (a, b) in enumerate(locals_)
    ]
    for copy in locals_:
        copy.start()

    barrier = pltpu.get_barrier_semaphore()
    others = [
        dev((x + 1) % X, y, z, c),
        dev((x + X - 1) % X, y, z, c),
        dev(x, (1 - yh) * YL + yl, z, c),
        dev(x, (1 - yh) * YL + 1 - yl, z, c),
    ]
    if X == 1:
        others = others[2:]
    for other in others:
        pl.semaphore_signal(barrier, inc=1, device_id=other, device_id_type=MESH)

    def greet(r, unused):
        pl.semaphore_signal(
            barrier, inc=1, device_id=((me + r) % blocks, t), device_id_type=MESH
        )
        return unused

    lax.fori_loop(1, blocks, greet, 0)
    pl.semaphore_wait(barrier, len(others) + blocks - 1)
    for copy in locals_:
        copy.wait()

    caches.run(0)
    asked.run(0)
    for piece in pieces:
        piece.run(0)
    column[...] = jnp.zeros(column.shape, jnp.float32)
    fresh = b_key.shape[0]
    count = k_all.shape[0] * k_all.shape[1] * k_all.shape[2]
    early = len(asked.steps)
    for step in range(1, early):
        caches.run(step)
        asked.run(step)
        for piece in pieces:
            piece.run(step)
    for step in range(early, len(caches.steps) + 1):
        caches.run(step)

    live = lax.broadcasted_iota(jnp.int32, (count, HD), 0) < lengths[me]
    keys = k_all[...].reshape(count, HD).astype(jnp.float32)
    values = v_all[...].reshape(count, HD).astype(jnp.float32)
    lead = jnp.broadcast_to(keys[0:1, :], (count, HD))
    k_buf[:count, :] = jnp.where(live, keys, lead).astype(jnp.bfloat16)
    v_buf[:count, :HD] = jnp.where(live, values, 0.0).astype(jnp.bfloat16)
    v_buf[:count, HD:] = jnp.where(live, 1.0, 0.0).astype(jnp.bfloat16)
    k_buf[count:count + fresh, :] = b_key[...]
    k_buf[count + fresh:, :] = jnp.zeros((HD - fresh, HD), jnp.bfloat16)
    v_buf[count:count + fresh, :HD] = b_value[...]
    v_buf[count + fresh:, :HD] = jnp.zeros((HD - fresh, HD), jnp.bfloat16)
    v_buf[count:, HD:] = jnp.ones((HD, HD), jnp.bfloat16)

    asked.run(early)
    asked.siblings()
    tiles = blocks // OWNERS
    tile_rows = OWNERS * fresh
    a_steps = max(len(piece.steps) for piece in pieces)
    late = {early: 0, early + 1: 1, early + 2: 2, early + 3: 6}

    def merge_copies(owner, source, target):
        return [
            pltpu.make_async_remote_copy(
                src_ref=a.at[source],
                dst_ref=b.at[target],
                send_sem=merge_send.at[i, source],
                recv_sem=merge_recv.at[i, target],
                device_id=(owner, t),
                device_id_type=MESH,
            )
            for i, (a, b) in enumerate(((part, part_in), (stat, stat_in)))
        ]

    def own_copies():
        return [
            pltpu.make_async_copy(a.at[me], b.at[me], local.at[i])
            for i, (a, b) in enumerate(((part, part_in), (stat, stat_in)))
        ]

    def tile_step(i, unused):
        for step in range(early, a_steps):
            @pl.when(i == min(late.get(step, tiles - 1), tiles - 1))
            def _():
                for piece in pieces:
                    piece.run(step)

        tile = (me // OWNERS + 1 + i) % tiles
        first = tile * OWNERS
        yl_at, z_at = first // (2 * Z), (first // 2) % Z
        q = q_all[yl_at, pl.ds(z_at, OWNERS // 2)].reshape(tile_rows, 2 * HD)
        bases, sums, outs = [], [], []
        for h in range(2):
            mine = q[:, h * HD:(h + 1) * HD]
            scores = dot(mine, k_buf[:count, :], NT)
            extra = dot(mine, k_buf[count:, :], NT)
            ki = lax.broadcasted_iota(jnp.int32, extra.shape, 1)
            ti = lax.broadcasted_iota(jnp.int32, extra.shape, 0) + first * fresh
            seen = jnp.logical_and(ki < fresh, ki + me * fresh <= ti)
            extra = jnp.where(seen, extra, LOWEST)
            top = jnp.maximum(
                jnp.max(scores, axis=1, keepdims=True), jnp.max(extra, axis=1, keepdims=True)
            )
            base = top * SCALE2
            p = jnp.exp2(scores * SCALE2 - base).astype(jnp.bfloat16)
            p_extra = jnp.exp2(extra * SCALE2 - base).astype(jnp.bfloat16)
            acc = dot(p, v_buf[:count, :], NN) + dot(p_extra, v_buf[count:, :], NN)
            outs.append((acc[:, :HD] / acc[:, HD:]).astype(jnp.bfloat16))
            bases.append(base)
            sums.append(acc[:, HD:HD + 1])
        lane = lax.broadcasted_iota(jnp.int32, (tile_rows, HD), 1)
        packed = jnp.where(
            lane == 0, bases[0], jnp.where(lane == 1, bases[1], jnp.where(lane == 2, sums[0], sums[1]))
        )
        column[:tile_rows, :] = packed
        for j in range(OWNERS):
            for h in range(2):
                part[first + j, :, h * HD:(h + 1) * HD] = outs[h][j * fresh:(j + 1) * fresh]
            stat[first + j] = column[j * fresh:j * fresh + HD, :].T[:8]
        for j in range(OWNERS):
            @pl.when(first + j != me)
            def _():
                for copy in merge_copies(first + j, first + j, me):
                    copy.start()

            @pl.when(first + j == me)
            def _():
                for copy in own_copies():
                    copy.start()

        return unused

    lax.fori_loop(0, tiles, tile_step, 0)
    for piece in pieces:
        piece.run(a_steps)
    for copy in own_copies():
        copy.wait()

    def arrive(r, unused):
        other = (me + r) % blocks
        for copy in merge_copies(other, other, other):
            copy.wait_recv()
        return unused

    lax.fori_loop(1, blocks, arrive, 0)
    for h in range(2):
        base = stat_in[:, h, :]
        best = jnp.max(base, axis=0, keepdims=True)
        share = stat_in[:, 2 + h, :] * jnp.exp2(base - best)
        share = jnp.concatenate(
            [share, jnp.zeros((HD - blocks, HD), jnp.float32)], axis=0
        ).T[:fresh]
        numer = jnp.zeros((fresh, HD), jnp.float32)
        for g in range(blocks):
            numer = numer + share[:, g:g + 1] * part_in[g, :, h * HD:(h + 1) * HD].astype(
                jnp.float32
            )
        denom = jnp.sum(share, axis=1, keepdims=True)
        b_out[:, h * HD:(h + 1) * HD] = (numer / denom).astype(jnp.bfloat16)
    for piece in pieces:
        piece.siblings()
    for copy in book.copies:
        copy.make().wait_send()

    def leave(r, unused):
        other = (me + r) % blocks
        for copy in merge_copies(other, other, other):
            copy.wait_send()
        return unused

    lax.fori_loop(1, blocks, leave, 0)


def exchange(blocks, heads, lengths, a_key, a_value, b_query, b_key, b_value, cache_key, cache_value):
    X, YH, YL, Z = sizes_of(blocks, heads)
    rows = a_key.shape[0]
    cut = rows * 3 // 4
    fresh = b_query.shape[0]
    slots = cache_key.shape[0]
    count = slots * heads

    def whole(height):
        return jax.ShapeDtypeStruct((YL, Z, 2, X, YH, height, HD), jnp.bfloat16)

    anywhere = pl.BlockSpec(memory_space=pl.ANY)
    vmem = pl.BlockSpec(memory_space=pltpu.VMEM)
    copies = 120
    return pl.pallas_call(
        functools.partial(exchange_kernel, blocks, heads),
        out_shape=(
            whole(cut),
            whole(cut),
            whole(rows - cut),
            whole(rows - cut),
            jax.ShapeDtypeStruct(b_query.shape, jnp.bfloat16),
        ),
        in_specs=[pl.BlockSpec(memory_space=pltpu.SMEM)]
        + [anywhere] * 3
        + [vmem] * 2
        + [anywhere] * 2,
        out_specs=[anywhere] * 4 + [vmem],
        scratch_shapes=[
            pltpu.VMEM((YL, Z, 2, fresh, 2 * HD), jnp.bfloat16),
            pltpu.VMEM((X, YH, slots, HD), jnp.bfloat16),
            pltpu.VMEM((X, YH, slots, HD), jnp.bfloat16),
            pltpu.VMEM((count + HD, HD), jnp.bfloat16),
            pltpu.VMEM((count + HD, 2 * HD), jnp.bfloat16),
            pltpu.VMEM((OWNERS * fresh + HD, HD), jnp.float32),
            pltpu.VMEM((blocks, fresh, 2 * HD), jnp.bfloat16),
            pltpu.VMEM((blocks, 8, HD), jnp.float32),
            pltpu.VMEM((blocks, fresh, 2 * HD), jnp.bfloat16),
            pltpu.VMEM((blocks, 8, HD), jnp.float32),
            pltpu.SemaphoreType.DMA((copies,)),
            pltpu.SemaphoreType.DMA((copies,)),
            pltpu.SemaphoreType.DMA((2, blocks)),
            pltpu.SemaphoreType.DMA((2, blocks)),
            pltpu.SemaphoreType.DMA((7,)),
        ],
        compiler_params=pltpu.CompilerParams(
            vmem_limit_bytes=40 * 2**20, collective_id=0, has_side_effects=True
        ),
        cost_estimate=pl.CostEstimate(
            flops=10_000_000_000, bytes_accessed=20_000_000, transcendentals=6_700_000
        ),
        name="exchange",
    )(lengths, a_key, a_value, b_query, b_key, b_value, cache_key, cache_value)


def a_kernel(
    shard_rows, pos_ref, q_ref, kx_ref, vy_ref, kz_ref, vz_ref, o_ref,
    k_buf, v_buf, m_buf, acc_buf, place, sems,
):
    total = kx_ref.shape[0]
    high = kx_ref.shape[1]
    group = lax.axis_index("blk")
    own = [pos_ref[2 * group], pos_ref[2 * group + 1]]
    first = (own[0] + CHUNK) // CHUNK
    steps = (total + CHUNK) // CHUNK

    def invert(i, unused):
        place[pos_ref[i]] = i
        return unused

    lax.fori_loop(0, total, invert, 0)

    def where_at(i):
        part = (i >= first).astype(jnp.int32)
        return part, i - part * first

    def fetch(i):
        part, at = where_at(i)
        slot = i % 2
        for b in range(CHUNK):
            block = place[at * CHUNK + b]
            for source, start, size in ((kx_ref, 0, high), (kz_ref, high, BLOCK - high)):
                pltpu.make_async_copy(
                    source.at[block], k_buf.at[slot, pl.ds(b * BLOCK + start, size)], sems.at[0, slot]
                ).start()
            for source, start, size in ((vy_ref, 0, high), (vz_ref, high, BLOCK - high)):
                pltpu.make_async_copy(
                    source.at[block],
                    v_buf.at[slot, pl.ds(b * BLOCK + start, size), pl.ds(0, HD)],
                    sems.at[1, slot],
                ).start()

    fetch(0)
    v_buf[:, :, HD:] = jnp.ones((2, CHUNK * BLOCK, HD), jnp.bfloat16)
    m_buf[...] = jnp.full(m_buf.shape, LOWEST, jnp.float32)
    acc_buf[...] = jnp.zeros(acc_buf.shape, jnp.float32)

    def step(i, unused):
        part, at = where_at(i)
        mine = jnp.where(part == 1, own[1], own[0])
        slot = i % 2

        @pl.when(i + 1 < steps)
        def _():
            fetch(i + 1)

        pltpu.make_async_copy(k_buf.at[slot], k_buf.at[slot], sems.at[0, slot]).wait()
        halves = v_buf.at[slot, :, pl.ds(0, HD)]
        pltpu.make_async_copy(halves, halves, sems.at[1, slot]).wait()

        def work(masked):
            for h in range(2):
                q = q_ref[pl.ds(pl.multiple_of(part * BLOCK, BLOCK), BLOCK), h * HD:(h + 1) * HD]
                s = dot(q, k_buf[slot], NT)
                if masked:
                    row = lax.broadcasted_iota(jnp.int32, (1, CHUNK * BLOCK), 1)
                    block = row // BLOCK
                    row = row % BLOCK
                    per = shard_rows * 3 // 4
                    rest = shard_rows - per
                    low = row - high
                    early, later = row, per + low
                    for n in range(1, BLOCK // shard_rows):
                        early = early + jnp.where(row >= per * n, rest, 0)
                        later = later + jnp.where(low >= rest * n, per, 0)
                    ki = jnp.where(row < high, early, later) + (block + at * CHUNK - mine) * BLOCK
                    qi = lax.broadcasted_iota(jnp.int32, s.shape, 0)
                    s = jnp.where(ki <= qi, s, LOWEST)
                old = m_buf[part, h]
                new = jnp.maximum(old, jnp.max(s, axis=1, keepdims=True))
                m_buf[part, h] = new
                factor = jnp.exp2((old - new) * SCALE2)
                p = jnp.exp2(s * SCALE2 - new[:, :1] * SCALE2).astype(jnp.bfloat16)
                acc_buf[part, h] = acc_buf[part, h] * factor[:, :1] + dot(p, v_buf[slot], NN)

        last = at == mine // CHUNK

        @pl.when(last)
        def _():
            work(True)

        @pl.when(jnp.logical_not(last))
        def _():
            work(False)

        return unused

    lax.fori_loop(0, steps, step, 0)
    for part in range(2):
        for h in range(2):
            acc = acc_buf[part, h]
            o_ref[part * BLOCK:(part + 1) * BLOCK, h * HD:(h + 1) * HD] = (
                acc[:, :HD] / acc[:, HD:]
            ).astype(jnp.bfloat16)


def attend_a(shard_rows, positions, queries, gathered):
    total = positions.shape[0]
    pieces = [g.reshape(total, -1, HD) for g in gathered]
    return pl.pallas_call(
        functools.partial(a_kernel, shard_rows),
        out_shape=jax.ShapeDtypeStruct(queries.shape, jnp.bfloat16),
        grid_spec=pltpu.PrefetchScalarGridSpec(
            num_scalar_prefetch=1,
            grid=(1,),
            in_specs=[pl.BlockSpec(queries.shape, lambda i, p: (0, 0))]
            + [pl.BlockSpec(memory_space=pl.ANY)] * 4,
            out_specs=pl.BlockSpec(queries.shape, lambda i, p: (0, 0)),
            scratch_shapes=[
                pltpu.VMEM((2, CHUNK * BLOCK, HD), jnp.bfloat16),
                pltpu.VMEM((2, CHUNK * BLOCK, 2 * HD), jnp.bfloat16),
                pltpu.VMEM((2, 2, BLOCK, HD), jnp.float32),
                pltpu.VMEM((2, 2, BLOCK, 2 * HD), jnp.float32),
                pltpu.SMEM((total,), jnp.int32),
                pltpu.SemaphoreType.DMA((2, 2)),
            ],
        ),
        compiler_params=pltpu.CompilerParams(vmem_limit_bytes=40 * 2**20),
        cost_estimate=pl.CostEstimate(
            flops=10_000_000_000, bytes_accessed=9_000_000, transcendentals=8_500_000
        ),
        name="attend_a",
    )(positions, queries, *pieces)


def shards(
    blocks,
    heads,
    a_query,
    a_key,
    a_value,
    b_query,
    b_key,
    b_value,
    cache_key,
    cache_value,
    a_positions,
    cache_lengths,
):
    *gathered, b_output = exchange(
        blocks, heads, cache_lengths, a_key, a_value, b_query, b_key, b_value, cache_key, cache_value
    )
    order = lax.slice(a_positions, (0,), a_positions.shape, (BLOCK,)) // BLOCK
    a_output = attend_a(a_key.shape[0], order, a_query, gathered)
    return (a_output, b_output)


def solution(mesh):
    in_specs = (
        P("blk", "tensor"),
        P(("blk", "tensor"), None),
        P(("blk", "tensor"), None),
        P("blk", "tensor"),
        P("blk", None),
        P("blk", None),
        P(("blk", "tensor"), None),
        P(("blk", "tensor"), None),
        P(),
        P(),
    )
    out_specs = (P("blk", "tensor"), P("blk", "tensor"))
    body = functools.partial(shards, mesh.shape["blk"], mesh.shape["tensor"])
    return jax.shard_map(body, mesh=mesh, in_specs=in_specs, out_specs=out_specs, check_vma=False)
```

time: 966 us -> 120 us (0.12)
  the two profiles are of different devices: /device:TPU:33 before, /device:TPU:9 now
where the time goes in v1:
time: 120 us
  Pallas kernels  111 us (92%)
  local copies, waits for them, and re-layouts  7.51 us (6%)
    pallas_call x1, Pallas kernels, exchange(): pl.pallas_call(functools.partial(exchange_kernel, blocks, heads), out_sha...  79.7 us
    pallas_call x1, Pallas kernels, attend_a(): pl.pallas_call(functools.partial(a_kernel, shard_rows), out_shape=jax.Sha...  31.6 us
    unnamed x19, local copies, waits for them, and re-layouts  6.53 us

profile of v1, /device:TPU:9, one launch (start us, length us, event | category | flops | bytes accessed | tf_op | source)
XLA Modules:
  0.0 119.5 jit_solution(4516287876606707234)
XLA Ops:
  0.6 1.0 slice.3
  1.6 0.0 copy-start.1
  1.6 0.8 copy-done.1
  2.5 0.0 copy-start.2
  2.5 0.8 copy-done.2
  3.3 0.0 copy-start.3
  3.3 0.7 copy-done.3
  4.0 0.0 copy-start.4
  4.0 0.7 copy-done.4
  4.8 0.0 copy-start.5
  4.8 0.7 copy-done.5
  5.5 0.0 copy-start.6
  5.5 0.7 copy-done.6
  6.2 0.0 copy-start.7
  6.2 0.7 copy-done.7
  6.9 0.0 copy-start.8
  6.9 0.7 copy-done.8
  7.6 0.0 copy-start
  7.6 79.7 %exchange.1 = (bf16[2,8,2,4,2,48,128]{6,5,4,3,2,1,0:T(8,128)(2,1)S(1)}, bf16[2,8,2,4,2,48,128]{6,5,4,3,2,1,0:T(8,128)(2,1)S(1)}, bf16[2,8,2,4,2,16,128]{6,5,4,3,...) custom-call(s32[32]{0:T(128)S(1)} %copy-done.8, ...), custom_call_target="tpu_custom_call" | custom-call | flops 10000000000 | bytes 20000000 | tf_op jit(solution)/shard_map/exchange/pallas_call | solution.py:402
  87.3 0.0 copy-done
  87.3 31.6 %attend_a.1 = bf16[512,256]{1,0:T(8,128)(2,1)} custom-call(s32[64]{0:T(128)S(1)} %and_select_fusion.pos_ref, bf16[512,256]{1,0:T(8,128)(2,1)S(1)} %copy-done, bf16[64,192,128]{2,1,0:T(8,128)(2,1)S(1)} %bitcast.4, bf16[64,192,128]{2,1,0:T(8,128)(2,1)S(1)} %bitcast.5, bf16[64,64,128]{2,1,0:T(8,128)(2,1)S(1)} %bitcast.6, bf16[64,64,128]{2,1,0:T(8,128)(2,1)S(1)} %bitcast.7), custom_call_target="tpu_custom_call" | custom-call | flops 10000000000 | bytes 9000000 | tf_op jit(solution)/shard_map/attend_a/pallas_call | solution.py:547
  118.9 0.6 copy.13
  (1 shorter events, 0.0 us)
Async XLA Ops:
  1.6 0.8 copy-start.1
  2.5 0.8 copy-start.2
  3.3 0.7 copy-start.3
  4.0 0.7 copy-start.4
  4.8 0.7 copy-start.5
  5.5 0.7 copy-start.6
  6.2 0.7 copy-start.7
  6.9 0.7 copy-start.8
  7.6 79.7 %copy-start = (bf16[512,256]{1,0:T(8,128)(2,1)S(1)}, bf16[512,256]{1,0:T(8,128)(2,1)}, u32[]{:S(2)}) copy-start(bf16[512,256]{1,0:T(8,128)(2,1)} %q_ref.1) | copy-start | bytes 786436

commit v2 on v1

v2 whole, which is shorter than its diff:
```python
import functools
import math

import jax
import jax.numpy as jnp
from jax import lax
from jax.experimental import pallas as pl
from jax.experimental.pallas import tpu as pltpu
from jax.sharding import PartitionSpec as P

HD = 128
BLOCK = 256
CHUNK = 4
OWNERS = 4
SCALE2 = HD ** (-0.5) * math.log2(math.e)
LOWEST = -1e30
NT = (((1,), (1,)), ((), ()))
NN = (((1,), (0,)), ((), ()))
MESH = pl.DeviceIdType.MESH


def dot(a, b, dims):
    return lax.dot_general(a, b, dims, preferred_element_type=jnp.float32)


class Copy:
    def __init__(self, book, view, device):
        self.book, self.view, self.device = book, view, device
        self.index = len(book.copies)
        book.copies.append(self)

    def make(self):
        return pltpu.make_async_remote_copy(
            src_ref=self.view(),
            dst_ref=self.view(),
            send_sem=self.book.send.at[self.index],
            recv_sem=self.book.recv.at[self.index],
            device_id=self.device,
            device_id_type=MESH,
        )


class Book:
    def __init__(self, send, recv):
        self.send, self.recv, self.copies = send, recv, []


class Gather:
    def __init__(self, book, views, order, axes, sibling):
        self.steps, self.forwards = [], []
        done = []
        for number, name in enumerate(order):
            axis = name.rstrip("*")
            size, at, device = axes[axis]
            final = number == len(order) - 1 and sibling is not None
            if final:
                self.forwards = [[] for step in self.steps]
                self.forwards.append(
                    [Copy(book, v, sibling) for v in views(tuple(done), axis, at, None)]
                )
            if name.endswith("*"):
                sends = []
                for way in range(1, size):
                    for v in views(tuple(done), axis, at, None):
                        sends.append(Copy(book, v, device(way)))
                if sends:
                    self.steps.append(sends)
                done.append(axis)
                continue
            for k in range(1, size // 2 + 1):
                sends, arrived = [], []
                for way in (1, -1):
                    if size == 2 and way == -1:
                        continue
                    half = None
                    if 2 * k == size and size > 2:
                        half = 0 if way == 1 else 1
                    out = (at - way * (k - 1) + 2 * size) % size
                    got = (at - way * k + 2 * size) % size
                    for v in views(tuple(done), axis, out, half):
                        sends.append(Copy(book, v, device(way)))
                    if final:
                        for v in views(tuple(done), axis, got, half):
                            arrived.append(Copy(book, v, sibling))
                self.steps.append(sends)
                if final:
                    self.forwards.append(arrived)
            done.append(axis)

    def run(self, step):
        if step > len(self.steps):
            return
        if step > 0:
            for copy in self.steps[step - 1]:
                copy.make().wait_recv()
        if step < len(self.steps):
            for copy in self.steps[step]:
                copy.make().start()
        if step < len(self.forwards):
            for copy in self.forwards[step]:
                copy.make().start()

    def siblings(self):
        for group in self.forwards:
            for copy in group:
                copy.make().wait_recv()


def sizes_of(blocks, heads):
    y_lo, y_hi = 2, 2
    return heads // y_hi, y_hi, y_lo, blocks // (2 * y_lo)


def exchange_kernel(
    blocks,
    heads,
    lengths_hbm,
    positions_hbm,
    a_key,
    a_value,
    b_query,
    b_key,
    b_value,
    cache_key,
    cache_value,
    key_all,
    value_all,
    part_in,
    stat_in,
    order,
    lengths,
    positions,
    q_all,
    k_all,
    v_all,
    k_buf,
    v_buf,
    part,
    col,
    part_near,
    col_near,
    held,
    held_col,
    column,
    part_out,
    stat_out,
    send,
    recv,
    near_send,
    near_recv,
    merge_send,
    merge_recv,
    local,
):
    X, YH, YL, Z = sizes_of(blocks, heads)
    Y = YH * YL
    me, t = lax.axis_index("blk"), lax.axis_index("tensor")
    yl, z, c = me // (2 * Z), (me // 2) % Z, me % 2
    x, yh = t // YH, t % YH
    y = yh * YL + yl
    mine = yl * Z + z
    chips = YL * Z

    def dev(x, y, z, c):
        return ((y % YL) * (2 * Z) + z * 2 + c, x * YH + y // YL)

    axes = {
        "x": (X, x, lambda way: dev((x + way + X) % X, y, z, c)),
        "y": (Y, y, lambda way: dev(x, (y + way + Y) % Y, z, c)),
        "z": (Z, z, lambda way: dev(x, y, (z + way + Z) % Z, c)),
        "yl": (YL, yl, lambda way: dev(x, yh * YL + (1 - yl), z, c)),
        "yh": (YH, yh, lambda way: dev(x, (1 - yh) * YL + yl, z, c)),
    }
    sibling = dev(x, y, z, 1 - c)
    every = slice(None)
    rows = a_key.shape[0]
    cut = rows * 3 // 4
    upper, lower = pl.ds(0, cut), pl.ds(cut, rows - cut)

    def a_views(arrays, lone):
        def views(done, axis, at, half):
            chosen = arrays
            zs = every if "z" in done else (at if axis == "z" else z)
            if half is not None:
                if len(arrays) == 2:
                    chosen = arrays[half:half + 1]
                elif "z" in done:
                    zs = pl.ds(half * (Z // 2), Z // 2)
                elif half != lone:
                    chosen = []
            xs = every if "x" in done else (at if axis == "x" else x)
            if "y" in done:
                yls, yhs = every, every
            elif axis == "y":
                yls, yhs = at % YL, at // YL
            else:
                yls, yhs = yl, yh
            return [lambda a=a, r=r: a.at[yls, zs, c, xs, yhs, r] for a, r in chosen]

        return views

    def near_views(done, axis, at, half):
        chosen = [k_all, v_all] if half is None else [k_all, v_all][half:half + 1]
        return [lambda a=a: a.at[yh, at] for a in chosen]

    def far_views(done, axis, at, half):
        chosen = [k_all, v_all] if half is None else [k_all, v_all][half:half + 1]
        if axis == "yh":
            return [lambda a=a: a.at[at, x] for a in chosen]
        return [lambda a=a: a.at[1 - yh, at] for a in chosen]

    def query_views(done, axis, at, half):
        if half == 1:
            return []
        yls = every if "yl" in done else (at if axis == "yl" else yl)
        zs = at if axis == "z" else z
        return [lambda: q_all.at[yls, zs, c]]

    book = Book(send, recv)
    near = Gather(book, near_views, ["x"], axes, None)
    far = Gather(book, far_views, ["yh", "x"], axes, None)
    asked = Gather(book, query_views, ["yl", "z"], axes, sibling)
    piece_x = Gather(book, a_views([(key_all, upper)], 0), ["z*", "y", "x"], axes, sibling)
    piece_y = Gather(book, a_views([(value_all, upper)], 1), ["z*", "x", "y"], axes, sibling)
    piece_z = Gather(
        book, a_views([(key_all, lower), (value_all, lower)], 0), ["x*", "y*", "z"], axes, sibling
    )

    fresh = b_query.shape[0]
    count = k_all.shape[1] * k_all.shape[2]
    locals_ = [
        (cache_key, k_all.at[yh, x]),
        (cache_value, v_all.at[yh, x]),
        (b_query, q_all.at[yl, z, c]),
        (a_key, key_all.at[yl, z, c, x, yh]),
        (a_value, value_all.at[yl, z, c, x, yh]),
        (b_key, k_buf.at[pl.ds(count, fresh)]),
        (b_value, v_buf.at[pl.ds(count, fresh), pl.ds(0, HD)]),
        (lengths_hbm, lengths),
        (positions_hbm, positions),
    ]
    locals_ = [
        pltpu.make_async_copy(a, b, local.at[i]) for i, (a, b) in enumerate(locals_)
    ]
    for copy in locals_:
        copy.start()

    barrier = pltpu.get_barrier_semaphore()
    others = [dev((x + r) % X, y, z, c) for r in range(1, X)] + [
        dev(x, (1 - yh) * YL + yl, z, c),
        dev(x, (1 - yh) * YL + 1 - yl, z, c),
        sibling,
    ]
    for other in others:
        pl.semaphore_signal(barrier, inc=1, device_id=other, device_id_type=MESH)

    def greet(r, unused):
        pl.semaphore_signal(
            barrier, inc=1, device_id=((me + 2 * r) % blocks, t), device_id_type=MESH
        )
        return unused

    lax.fori_loop(1, chips, greet, 0)
    pl.semaphore_wait(barrier, len(others) + chips - 1)
    for copy in locals_:
        copy.wait()

    far.run(0)
    near.run(0)
    asked.run(0)
    piece_z.run(0)
    piece_x.run(0)
    piece_y.run(0)
    column[...] = jnp.zeros(column.shape, jnp.float32)
    k_buf[count + fresh:, :] = jnp.zeros((HD - fresh, HD), jnp.bfloat16)
    v_buf[count + fresh:, :HD] = jnp.zeros((HD - fresh, HD), jnp.bfloat16)
    v_buf[count:, HD:] = jnp.ones((HD, HD), jnp.bfloat16)
    asked.run(1)
    asked.run(2)
    near.run(1)
    piece_z.run(1)
    piece_x.run(1)
    piece_y.run(1)
    asked.run(3)
    far.run(1)
    piece_z.run(2)
    asked.run(4)
    near.run(2)

    def label(i, unused):
        order[i] = positions[i * BLOCK] // BLOCK
        return unused

    lax.fori_loop(0, order.shape[0], label, 0)
    slots = k_all.shape[2]
    side = X * slots
    limit = lengths[me]

    def prepare(which, lead):
        row = lax.broadcasted_iota(jnp.int32, (side, HD), 0)
        live = (row // slots) * (YH * slots) + row % slots + which * slots < limit
        keys = k_all[which].reshape(side, HD).astype(jnp.float32)
        values = v_all[which].reshape(side, HD).astype(jnp.float32)
        lead = jnp.broadcast_to(lead, (side, HD))
        k_buf[:side, :] = jnp.where(live, keys, lead).astype(jnp.bfloat16)
        v_buf[:side, :HD] = jnp.where(live, values, 0.0).astype(jnp.bfloat16)
        v_buf[:side, HD:] = jnp.where(live, 1.0, 0.0).astype(jnp.bfloat16)

    prepare(yh, k_all[yh, 0][:1].astype(jnp.float32))
    piece_x.run(2)
    piece_y.run(2)
    asked.run(5)
    asked.siblings()

    tiles = blocks // OWNERS
    zs_tile = OWNERS // 2
    tile_rows = OWNERS * fresh
    late = [
        (0, piece_z, 4), (2, piece_z, 5), (4, piece_x, 4), (4, piece_y, 4), (6, piece_z, 6),
    ]
    soon = [(1, far, 2), (3, piece_x, 3), (3, piece_y, 3), (4, piece_z, 3)]

    def tile_of(i):
        first = ((me // OWNERS + 1 + i) % tiles) * OWNERS
        return first, first // (2 * Z), (first // 2) % Z

    def near_copies(i):
        return [
            pltpu.make_async_remote_copy(
                src_ref=a.at[i, 1 - c],
                dst_ref=b.at[i],
                send_sem=near_send.at[n, i],
                recv_sem=near_recv.at[n, i],
                device_id=sibling,
                device_id_type=MESH,
            )
            for n, (a, b) in enumerate(((part, part_near), (col, col_near)))
        ]

    def merge_copies(source, slot, owner, sem):
        return [
            pltpu.make_async_remote_copy(
                src_ref=a.at[source],
                dst_ref=b.at[slot],
                send_sem=merge_send.at[n, sem],
                recv_sem=merge_recv.at[n, slot],
                device_id=(owner, t),
                device_id_type=MESH,
            )
            for n, (a, b) in enumerate(((part_out, part_in), (stat_out, stat_in)))
        ]

    def own_copies(source):
        return [
            pltpu.make_async_copy(a.at[source], b.at[mine], local.at[n])
            for n, (a, b) in enumerate(((part_out, part_in), (stat_out, stat_in)))
        ]

    lane = lax.broadcasted_iota(jnp.int32, (fresh, HD), 1)

    def finish(i):
        for copy in near_copies(i):
            copy.wait_recv()
        first, yl_at, z_at = tile_of(i)
        for n in range(zs_tile):
            ours, theirs = col[i, c, n], col_near[i, n]
            stats = []
            for h in range(2):
                base0, base1 = ours[:, h:h + 1], theirs[:, h:h + 1]
                base = jnp.maximum(base0, base1)
                share0 = ours[:, 2 + h:3 + h] * jnp.exp2(base0 - base)
                share1 = theirs[:, 2 + h:3 + h] * jnp.exp2(base1 - base)
                total = share0 + share1
                at = slice(h * HD, (h + 1) * HD)
                both = share0 * part[i, c, n, :, at].astype(jnp.float32) + share1 * part_near[
                    i, n, :, at
                ].astype(jnp.float32)
                part_out[zs_tile * i + n, :, at] = (both / total).astype(jnp.bfloat16)
                stats += [base, total]
            column[:fresh, :] = jnp.where(
                lane == 0,
                stats[0],
                jnp.where(lane == 1, stats[2], jnp.where(lane == 2, stats[1], stats[3])),
            )
            stat_out[zs_tile * i + n] = column[...].T[:8]
        for n in range(zs_tile):
            owner = first + 2 * n + c
            slot = yl_at * Z + z_at + n

            @pl.when(owner != me)
            def _():
                for copy in merge_copies(zs_tile * i + n, mine, owner, slot):
                    copy.start()

            @pl.when(owner == me)
            def _():
                for copy in own_copies(zs_tile * i + n):
                    copy.start()

    wide = lax.broadcasted_iota(jnp.int32, (tile_rows, HD), 1)

    def pack(bases, sums):
        return jnp.where(
            wide == 0, bases[0], jnp.where(wide == 1, bases[1], jnp.where(wide == 2, sums[0], sums[1]))
        )

    def near_step(i, unused):
        for at, piece, step in soon:
            @pl.when(i == min(at, tiles - 1))
            def _():
                piece.run(step)

        first, yl_at, z_at = tile_of(i)
        q = q_all[yl_at, pl.ds(z_at, zs_tile)].reshape(tile_rows, 2 * HD)
        bases, sums = [], []
        for h in range(2):
            scores = dot(q[:, h * HD:(h + 1) * HD], k_buf[:side, :], NT)
            base = jnp.max(scores, axis=1, keepdims=True) * SCALE2
            p = jnp.exp2(scores * SCALE2 - base).astype(jnp.bfloat16)
            acc = dot(p, v_buf[:side, :], NN)
            held[i, :, h * HD:(h + 1) * HD] = acc[:, :HD]
            bases.append(jnp.where(yh * slots < limit, base, LOWEST))
            sums.append(acc[:, HD:HD + 1])
        held_col[i] = pack(bases, sums)
        return unused

    lax.fori_loop(0, tiles, near_step, 0)
    far.run(3)
    prepare(1 - yh, k_all[0, 0][:1].astype(jnp.float32))

    def tile_step(i, unused):
        for at, piece, step in late:
            @pl.when(i == min(at, tiles - 1))
            def _():
                piece.run(step)

        first, yl_at, z_at = tile_of(i)
        q = q_all[yl_at, pl.ds(z_at, zs_tile)].reshape(tile_rows, 2 * HD)
        before = held_col[i]
        bases, sums, outs = [], [], []
        for h in range(2):
            mine_q = q[:, h * HD:(h + 1) * HD]
            scores = dot(mine_q, k_buf[:side, :], NT)
            extra = dot(mine_q, k_buf[side:, :], NT)
            ki = lax.broadcasted_iota(jnp.int32, extra.shape, 1)
            ti = lax.broadcasted_iota(jnp.int32, extra.shape, 0) + first * fresh
            seen = jnp.logical_and(ki < fresh, ki + me * fresh <= ti)
            extra = jnp.where(seen, extra, LOWEST)
            top = jnp.maximum(
                jnp.max(scores, axis=1, keepdims=True), jnp.max(extra, axis=1, keepdims=True)
            )
            old = before[:, h:h + 1]
            base = jnp.maximum(old, top * SCALE2)
            factor = jnp.exp2(old - base)
            p = jnp.exp2(scores * SCALE2 - base).astype(jnp.bfloat16)
            p_extra = jnp.exp2(extra * SCALE2 - base).astype(jnp.bfloat16)
            acc = dot(p, v_buf[:side, :], NN) + dot(p_extra, v_buf[side:, :], NN)
            total = acc[:, HD:HD + 1] + before[:, 2 + h:3 + h] * factor
            outs.append(
                ((acc[:, :HD] + held[i, :, h * HD:(h + 1) * HD] * factor) / total).astype(
                    jnp.bfloat16
                )
            )
            bases.append(base)
            sums.append(total)
        packed = pack(bases, sums)
        for j in range(OWNERS):
            at = slice(j * fresh, (j + 1) * fresh)
            for h in range(2):
                part[i, j % 2, j // 2, :, h * HD:(h + 1) * HD] = outs[h][at]
            col[i, j % 2, j // 2] = packed[at]
        for copy in near_copies(i):
            copy.start()

        @pl.when(i > 0)
        def _():
            finish(i - 1)

        return unused

    lax.fori_loop(0, tiles, tile_step, 0)
    finish(tiles - 1)
    piece_x.run(5)
    piece_y.run(5)
    for copy in own_copies(0):
        copy.wait()

    def arrive(r, unused):
        other = (mine + r) % chips
        for copy in merge_copies(0, other, 2 * other + c, other):
            copy.wait_recv()
        return unused

    lax.fori_loop(1, chips, arrive, 0)
    for piece in (piece_x, piece_y, piece_z):
        piece.siblings()
    for copy in book.copies:
        copy.make().wait_send()

    def leave(r, unused):
        other = (mine + r) % chips
        for copy in merge_copies(0, other, 2 * other + c, other):
            copy.wait_send()
        return unused

    lax.fori_loop(1, chips, leave, 0)

    def part_ways(i, unused):
        for copy in near_copies(i):
            copy.wait_send()
        return unused

    lax.fori_loop(0, tiles, part_ways, 0)


def exchange(blocks, heads, lengths, positions, a_key, a_value, b_query, b_key, b_value, cache_key, cache_value):
    X, YH, YL, Z = sizes_of(blocks, heads)
    rows = a_key.shape[0]
    fresh = b_query.shape[0]
    slots = cache_key.shape[0]
    count = slots * X
    chips = YL * Z
    tiles = blocks // OWNERS
    half = OWNERS // 2
    whole = jax.ShapeDtypeStruct((YL, Z, 2, X, YH, rows, HD), jnp.bfloat16)
    hbm = pl.BlockSpec(memory_space=pltpu.HBM)
    anywhere = pl.BlockSpec(memory_space=pl.ANY)
    copies = 128
    return pl.pallas_call(
        functools.partial(exchange_kernel, blocks, heads),
        out_shape=(
            whole,
            whole,
            jax.ShapeDtypeStruct((chips, fresh, 2 * HD), jnp.bfloat16),
            jax.ShapeDtypeStruct((chips, 8, HD), jnp.float32),
            jax.ShapeDtypeStruct((positions.shape[0] // BLOCK,), jnp.int32),
        ),
        in_specs=[hbm] * 9,
        out_specs=[anywhere] * 4 + [pl.BlockSpec(memory_space=pltpu.SMEM)],
        scratch_shapes=[
            pltpu.SMEM(lengths.shape, jnp.int32),
            pltpu.SMEM(positions.shape, jnp.int32),
            pltpu.VMEM((YL, Z, 2, fresh, 2 * HD), jnp.bfloat16),
            pltpu.VMEM((YH, X, slots, HD), jnp.bfloat16),
            pltpu.VMEM((YH, X, slots, HD), jnp.bfloat16),
            pltpu.VMEM((count + HD, HD), jnp.bfloat16),
            pltpu.VMEM((count + HD, 2 * HD), jnp.bfloat16),
            pltpu.VMEM((tiles, 2, half, fresh, 2 * HD), jnp.bfloat16),
            pltpu.VMEM((tiles, 2, half, fresh, HD), jnp.float32),
            pltpu.VMEM((tiles, half, fresh, 2 * HD), jnp.bfloat16),
            pltpu.VMEM((tiles, half, fresh, HD), jnp.float32),
            pltpu.VMEM((tiles, OWNERS * fresh, 2 * HD), jnp.float32),
            pltpu.VMEM((tiles, OWNERS * fresh, HD), jnp.float32),
            pltpu.VMEM((HD, HD), jnp.float32),
            pltpu.VMEM((chips, fresh, 2 * HD), jnp.bfloat16),
            pltpu.VMEM((chips, 8, HD), jnp.float32),
            pltpu.SemaphoreType.DMA((copies,)),
            pltpu.SemaphoreType.DMA((copies,)),
            pltpu.SemaphoreType.DMA((2, tiles)),
            pltpu.SemaphoreType.DMA((2, tiles)),
            pltpu.SemaphoreType.DMA((2, chips)),
            pltpu.SemaphoreType.DMA((2, chips)),
            pltpu.SemaphoreType.DMA((9,)),
        ],
        compiler_params=pltpu.CompilerParams(
            vmem_limit_bytes=32 * 2**20, collective_id=0, has_side_effects=True
        ),
        cost_estimate=pl.CostEstimate(
            flops=10_000_000_000, bytes_accessed=20_000_000, transcendentals=6_700_000
        ),
        name="exchange",
    )(
        *[
            pltpu.with_memory_space_constraint(v, pltpu.HBM)
            for v in (
                lengths, positions, a_key, a_value, b_query, b_key, b_value, cache_key, cache_value
            )
        ]
    )


def a_kernel(
    fresh, pos_ref, q_ref, key_ref, value_ref, part_ref, stat_ref, o_ref, b_ref,
    q_buf, m_buf, acc_buf, place,
):
    total = key_ref.shape[0]
    chips = part_ref.shape[0]
    group = lax.axis_index("blk")
    own = [pos_ref[2 * group], pos_ref[2 * group + 1]]
    wholes = own[0] // CHUNK
    steps = total // CHUNK - 1
    unroll = 3 if steps % 3 == 0 else 1

    def invert(i, unused):
        place[pos_ref[i]] = i
        return unused

    lax.fori_loop(0, total, invert, 0)
    ones = jnp.ones((CHUNK * BLOCK, HD), jnp.bfloat16)
    for part in range(2):
        for h in range(2):
            q = q_ref[part * BLOCK:(part + 1) * BLOCK, h * HD:(h + 1) * HD]
            q = q.astype(jnp.float32) * SCALE2
            main = q.astype(jnp.bfloat16)
            q_buf[part, h, :, :HD] = main
            q_buf[part, h, :, HD:] = (q - main.astype(jnp.float32)).astype(jnp.bfloat16)

    def load(at):
        where = [place[at * CHUNK + b] for b in range(CHUNK)]
        keys = jnp.concatenate([key_ref[w] for w in where], axis=0)
        values = jnp.concatenate([value_ref[w] for w in where], axis=0)
        return jnp.concatenate([keys, keys], axis=1), jnp.concatenate([values, ones], axis=1)

    for part in range(2):
        at = own[part] // CHUNK
        keys, values = load(at)
        for h in range(2):
            s = dot(q_buf[part, h], keys, NT)
            ki = lax.broadcasted_iota(jnp.int32, s.shape, 1) + (at * CHUNK - own[part]) * BLOCK
            qi = lax.broadcasted_iota(jnp.int32, s.shape, 0)
            s = jnp.where(ki <= qi, s, LOWEST)
            new = jnp.max(s, axis=1, keepdims=True)
            m_buf[part, h] = jnp.broadcast_to(new, (BLOCK, HD))
            p = jnp.exp2(s - new).astype(jnp.bfloat16)
            acc_buf[part, h] = dot(p, values, NN)

    def step(j, unused):
        for n in range(unroll):
            i = j * unroll + n
            part = (i >= wholes).astype(jnp.int32)
            keys, values = load(i - part * wholes)
            for h in range(2):
                s = dot(q_buf[part, h], keys, NT)
                old = m_buf[part, h]
                new = jnp.maximum(old, jnp.max(s, axis=1, keepdims=True))
                m_buf[part, h] = new
                factor = jnp.exp2(old - new)
                p = jnp.exp2(s - new[:, :1]).astype(jnp.bfloat16)
                acc_buf[part, h] = acc_buf[part, h] * factor[:, :1] + dot(p, values, NN)
        return unused

    lax.fori_loop(0, steps // unroll, step, 0)
    for part in range(2):
        for h in range(2):
            acc = acc_buf[part, h]
            o_ref[part * BLOCK:(part + 1) * BLOCK, h * HD:(h + 1) * HD] = (
                acc[:, :HD] / acc[:, HD:]
            ).astype(jnp.bfloat16)

    for h in range(2):
        base = stat_ref[:, h, :]
        best = jnp.max(base, axis=0, keepdims=True)
        share = stat_ref[:, 2 + h, :] * jnp.exp2(base - best)
        share = jnp.concatenate(
            [share, jnp.zeros((HD - chips, HD), jnp.float32)], axis=0
        ).T[:fresh]
        numer = jnp.zeros((fresh, HD), jnp.float32)
        for g in range(chips):
            numer = numer + share[:, g:g + 1] * part_ref[g, :, h * HD:(h + 1) * HD].astype(
                jnp.float32
            )
        denom = jnp.sum(share, axis=1, keepdims=True)
        b_ref[:, h * HD:(h + 1) * HD] = (numer / denom).astype(jnp.bfloat16)


def attend_a(fresh, positions, queries, keys, values, part, stat):
    total = positions.shape[0]
    vmem = pl.BlockSpec(memory_space=pltpu.VMEM)
    return pl.pallas_call(
        functools.partial(a_kernel, fresh),
        out_shape=(
            jax.ShapeDtypeStruct(queries.shape, jnp.bfloat16),
            jax.ShapeDtypeStruct((fresh, 2 * HD), jnp.bfloat16),
        ),
        in_specs=[pl.BlockSpec(memory_space=pltpu.SMEM)] + [vmem] * 5,
        out_specs=[vmem, vmem],
        scratch_shapes=[
            pltpu.VMEM((2, 2, BLOCK, 2 * HD), jnp.bfloat16),
            pltpu.VMEM((2, 2, BLOCK, HD), jnp.float32),
            pltpu.VMEM((2, 2, BLOCK, 2 * HD), jnp.float32),
            pltpu.SMEM((total,), jnp.int32),
        ],
        compiler_params=pltpu.CompilerParams(vmem_limit_bytes=32 * 2**20),
        cost_estimate=pl.CostEstimate(
            flops=10_000_000_000, bytes_accessed=9_000_000, transcendentals=8_500_000
        ),
        name="attend_a",
    )(positions, queries, keys.reshape(total, -1, HD), values.reshape(total, -1, HD), part, stat)


def shards(
    blocks,
    heads,
    a_query,
    a_key,
    a_value,
    b_query,
    b_key,
    b_value,
    cache_key,
    cache_value,
    a_positions,
    cache_lengths,
):
    *gathered, order = exchange(
        blocks,
        heads,
        cache_lengths,
        a_positions,
        a_key,
        a_value,
        b_query,
        b_key,
        b_value,
        cache_key,
        cache_value,
    )
    return attend_a(b_query.shape[0], order, a_query, *gathered)


def solution(mesh):
    in_specs = (
        P("blk", "tensor"),
        P(("blk", "tensor"), None),
        P(("blk", "tensor"), None),
        P("blk", "tensor"),
        P("blk", None),
        P("blk", None),
        P(("blk", "tensor"), None),
        P(("blk", "tensor"), None),
        P(),
        P(),
    )
    out_specs = (P("blk", "tensor"), P("blk", "tensor"))
    body = functools.partial(shards, mesh.shape["blk"], mesh.shape["tensor"])
    return jax.shard_map(body, mesh=mesh, in_specs=in_specs, out_specs=out_specs, check_vma=False)
```

time: 120 us -> 83.5 us (0.70)
  the two profiles are of different devices: /device:TPU:9 before, /device:TPU:1 now
where the time goes in v2:
time: 83.5 us; the launch traced here: 83.4 us
  Pallas kernels  82.7 us (99%)
    pallas_call x1, Pallas kernels, exchange(): pl.pallas_call(functools.partial(exchange_kernel, blocks, heads), out_sha...  65.8 us
    pallas_call x1, Pallas kernels, attend_a(): pl.pallas_call(functools.partial(a_kernel, fresh), out_shape=(jax.ShapeDt...  16.9 us

profile of v2, /device:TPU:1, one launch (start us, length us, event | category | flops | bytes accessed | tf_op | source)
XLA Modules:
  0.0 83.4 jit_solution(2820640750931834988)
XLA Ops:
  0.6 0.0 copy-start
  0.6 65.8 %exchange.1 = (bf16[2,8,2,4,2,64,128]{6,5,4,3,2,1,0:T(8,128)(2,1)S(1)}, bf16[2,8,2,4,2,64,128]{6,5,4,3,2,1,0:T(8,128)(2,1)S(1)}, bf16[16,48,256]{2,1,0:T(8,128)(...) custom-call(s32[32]{0:T(128)} %lengths_hbm.1, s32[16384]{0:T(1024)} %positions_hbm.1, bf16[64,128]{1,0:T(8,128)(2,1)} %a_key.1, ...), custom_call_target="tpu_custom_call" | custom-call | flops 10000000000 | bytes 20000000 | tf_op jit(solution)/shard_map/exchange/pallas_call | solution.py:529
  66.5 0.0 copy-done
  66.5 16.9 %attend_a.1 = (bf16[512,256]{1,0:T(8,128)(2,1)}, bf16[48,256]{1,0:T(8,128)(2,1)}) custom-call(s32[64]{0:T(128)S(1)} %get-tuple-element.7.pos_ref, bf16[512,256]{1,0:T(8,128)(2,1)S(1)} %copy-done, bf16[64,256,128]{2,1,0:T(8,128)(2,1)S(1)} %bitcast.2, bf16[64,256,128]{2,1,0:T(8,128)(2,1)S(1)} %bitcast.3, bf16[16,48,256]{2,1,0:T(8,128)(2,1)S(1)} %get-tuple-element.10.part_ref, ...), custom_call_target="tpu_custom_call" | custom-call | flops 10000000000 | bytes 9000000 | tf_op jit(solution)/shard_map/attend_a/pallas_call | solution.py:669
Async XLA Ops:
  0.6 65.8 %copy-start = (bf16[512,256]{1,0:T(8,128)(2,1)S(1)}, bf16[512,256]{1,0:T(8,128)(2,1)}, u32[]{:S(2)}) copy-start(bf16[512,256]{1,0:T(8,128)(2,1)} %q_ref.1) | copy-start | bytes 786436

commit v3 on v2

--- a/solution.py
+++ b/solution.py
@@ -100,8 +100,8 @@
             for copy in self.forwards[step]:
                 copy.make().start()
 
-    def siblings(self):
-        for group in self.forwards:
+    def siblings(self, first=0, last=99):
+        for group in self.forwards[first:last]:
             for copy in group:
                 copy.make().wait_recv()
 
@@ -262,7 +262,7 @@
 
     lax.fori_loop(1, chips, greet, 0)
     pl.semaphore_wait(barrier, len(others) + chips - 1)
-    for copy in locals_:
+    for copy in locals_[:-1]:
         copy.wait()
 
     far.run(0)
@@ -276,22 +276,14 @@
     v_buf[count + fresh:, :HD] = jnp.zeros((HD - fresh, HD), jnp.bfloat16)
     v_buf[count:, HD:] = jnp.ones((HD, HD), jnp.bfloat16)
     asked.run(1)
-    asked.run(2)
-    near.run(1)
     piece_z.run(1)
     piece_x.run(1)
     piece_y.run(1)
-    asked.run(3)
+    near.run(1)
+    asked.run(2)
+    piece_z.run(2)
     far.run(1)
-    piece_z.run(2)
-    asked.run(4)
     near.run(2)
-
-    def label(i, unused):
-        order[i] = positions[i * BLOCK] // BLOCK
-        return unused
-
-    lax.fori_loop(0, order.shape[0], label, 0)
     slots = k_all.shape[2]
     side = X * slots
     limit = lengths[me]
@@ -307,22 +299,46 @@
         v_buf[:side, HD:] = jnp.where(live, 1.0, 0.0).astype(jnp.bfloat16)
 
     prepare(yh, k_all[yh, 0][:1].astype(jnp.float32))
-    piece_x.run(2)
-    piece_y.run(2)
-    asked.run(5)
-    asked.siblings()
+    asked.siblings(0, 3)
 
     tiles = blocks // OWNERS
     zs_tile = OWNERS // 2
     tile_rows = OWNERS * fresh
+    soon = [
+        (0, lambda: asked.run(3)),
+        (0, lambda: piece_x.run(2)),
+        (0, lambda: piece_y.run(2)),
+        (1, lambda: asked.run(4)),
+        (1, lambda: piece_z.run(3)),
+        (2, lambda: asked.siblings(3, 5)),
+        (2, lambda: far.run(2)),
+        (3, lambda: asked.run(5)),
+        (3, lambda: piece_x.run(3)),
+        (3, lambda: piece_y.run(3)),
+        (4, lambda: piece_z.run(4)),
+        (6, lambda: asked.siblings(5)),
+    ]
     late = [
-        (0, piece_z, 4), (2, piece_z, 5), (4, piece_x, 4), (4, piece_y, 4), (6, piece_z, 6),
+        (0, lambda: piece_z.run(5)),
+        (3, lambda: piece_z.run(6)),
+        (4, lambda: piece_x.run(4)),
+        (4, lambda: piece_y.run(4)),
     ]
-    soon = [(1, far, 2), (3, piece_x, 3), (3, piece_y, 3), (4, piece_z, 3)]
+
+    def serve(i, todo):
+        for at in range(tiles):
+            now = [act for when, act in todo if min(when, tiles - 1) == at]
+            if now:
+                @pl.when(i == at)
+                def _():
+                    for act in now:
+                        act()
 
     def tile_of(i):
-        first = ((me // OWNERS + 1 + i) % tiles) * OWNERS
-        return first, first // (2 * Z), (first // 2) % Z
+        pairs, k = Z // 2, i // 2
+        away = ((k + 1) // 2) * (2 * (k % 2) - 1)
+        yl_at, z_at = (yl + i) % 2, ((z // 2 + away + pairs) % pairs) * 2
+        return yl_at * (2 * Z) + 2 * z_at, yl_at, z_at
 
     def near_copies(i):
         return [
@@ -340,20 +356,24 @@
     def merge_copies(source, slot, owner, sem):
         return [
             pltpu.make_async_remote_copy(
-                src_ref=a.at[source],
+                src_ref=a,
                 dst_ref=b.at[slot],
                 send_sem=merge_send.at[n, sem],
                 recv_sem=merge_recv.at[n, slot],
                 device_id=(owner, t),
                 device_id_type=MESH,
             )
-            for n, (a, b) in enumerate(((part_out, part_in), (stat_out, stat_in)))
+            for n, (a, b) in enumerate(
+                ((part_out.at[source], part_in), (stat_out.at[source // zs_tile], stat_in))
+            )
         ]
 
     def own_copies(source):
         return [
-            pltpu.make_async_copy(a.at[source], b.at[mine], local.at[n])
-            for n, (a, b) in enumerate(((part_out, part_in), (stat_out, stat_in)))
+            pltpu.make_async_copy(a, b.at[mine], local.at[n])
+            for n, (a, b) in enumerate(
+                ((part_out.at[source], part_in), (stat_out.at[source // zs_tile], stat_in))
+            )
         ]
 
     lane = lax.broadcasted_iota(jnp.int32, (fresh, HD), 1)
@@ -377,12 +397,12 @@
                 ].astype(jnp.float32)
                 part_out[zs_tile * i + n, :, at] = (both / total).astype(jnp.bfloat16)
                 stats += [base, total]
-            column[:fresh, :] = jnp.where(
+            column[n * (HD // 2):n * (HD // 2) + fresh, :] = jnp.where(
                 lane == 0,
                 stats[0],
                 jnp.where(lane == 1, stats[2], jnp.where(lane == 2, stats[1], stats[3])),
             )
-            stat_out[zs_tile * i + n] = column[...].T[:8]
+        stat_out[i] = column[...].T[:8]
         for n in range(zs_tile):
             owner = first + 2 * n + c
             slot = yl_at * Z + z_at + n
@@ -405,16 +425,13 @@
         )
 
     def near_step(i, unused):
-        for at, piece, step in soon:
-            @pl.when(i == min(at, tiles - 1))
-            def _():
-                piece.run(step)
+        serve(i, soon)
 
         first, yl_at, z_at = tile_of(i)
         q = q_all[yl_at, pl.ds(z_at, zs_tile)].reshape(tile_rows, 2 * HD)
         bases, sums = [], []
-        for h in range(2):
-            scores = dot(q[:, h * HD:(h + 1) * HD], k_buf[:side, :], NT)
+        both = [dot(q[:, h * HD:(h + 1) * HD], k_buf[:side, :], NT) for h in range(2)]
+        for h, scores in enumerate(both):
             base = jnp.max(scores, axis=1, keepdims=True) * SCALE2
             p = jnp.exp2(scores * SCALE2 - base).astype(jnp.bfloat16)
             acc = dot(p, v_buf[:side, :], NN)
@@ -426,22 +443,30 @@
 
     lax.fori_loop(0, tiles, near_step, 0)
     far.run(3)
+    locals_[-1].wait()
+
+    def label(i, unused):
+        order[i] = positions[i * BLOCK] // BLOCK
+        return unused
+
+    lax.fori_loop(0, order.shape[0], label, 0)
     prepare(1 - yh, k_all[0, 0][:1].astype(jnp.float32))
 
     def tile_step(i, unused):
-        for at, piece, step in late:
-            @pl.when(i == min(at, tiles - 1))
-            def _():
-                piece.run(step)
+        serve(i, late)
 
         first, yl_at, z_at = tile_of(i)
         q = q_all[yl_at, pl.ds(z_at, zs_tile)].reshape(tile_rows, 2 * HD)
         before = held_col[i]
         bases, sums, outs = [], [], []
-        for h in range(2):
-            mine_q = q[:, h * HD:(h + 1) * HD]
-            scores = dot(mine_q, k_buf[:side, :], NT)
-            extra = dot(mine_q, k_buf[side:, :], NT)
+        both = [
+            (
+                dot(q[:, h * HD:(h + 1) * HD], k_buf[:side, :], NT),
+                dot(q[:, h * HD:(h + 1) * HD], k_buf[side:, :], NT),
+            )
+            for h in range(2)
+        ]
+        for h, (scores, extra) in enumerate(both):
             ki = lax.broadcasted_iota(jnp.int32, extra.shape, 1)
             ti = lax.broadcasted_iota(jnp.int32, extra.shape, 0) + first * fresh
             seen = jnp.logical_and(ki < fresh, ki + me * fresh <= ti)
@@ -553,7 +578,7 @@
             pltpu.VMEM((tiles, OWNERS * fresh, HD), jnp.float32),
             pltpu.VMEM((HD, HD), jnp.float32),
             pltpu.VMEM((chips, fresh, 2 * HD), jnp.bfloat16),
-            pltpu.VMEM((chips, 8, HD), jnp.float32),
+            pltpu.VMEM((tiles, 8, HD), jnp.float32),
             pltpu.SemaphoreType.DMA((copies,)),
             pltpu.SemaphoreType.DMA((copies,)),
             pltpu.SemaphoreType.DMA((2, tiles)),
@@ -581,7 +606,7 @@
 
 def a_kernel(
     fresh, pos_ref, q_ref, key_ref, value_ref, part_ref, stat_ref, o_ref, b_ref,
-    q_buf, m_buf, acc_buf, place,
+    q_buf, s_buf, m_buf, acc_buf, place,
 ):
     total = key_ref.shape[0]
     chips = part_ref.shape[0]
@@ -605,15 +630,17 @@
             q_buf[part, h, :, :HD] = main
             q_buf[part, h, :, HD:] = (q - main.astype(jnp.float32)).astype(jnp.bfloat16)
 
-    def load(at):
-        where = [place[at * CHUNK + b] for b in range(CHUNK)]
-        keys = jnp.concatenate([key_ref[w] for w in where], axis=0)
-        values = jnp.concatenate([value_ref[w] for w in where], axis=0)
-        return jnp.concatenate([keys, keys], axis=1), jnp.concatenate([values, ones], axis=1)
+    def load_keys(at):
+        keys = jnp.concatenate([key_ref[place[at * CHUNK + b]] for b in range(CHUNK)], axis=0)
+        return jnp.concatenate([keys, keys], axis=1)
+
+    def load_values(at):
+        values = jnp.concatenate([value_ref[place[at * CHUNK + b]] for b in range(CHUNK)], axis=0)
+        return jnp.concatenate([values, ones], axis=1)
 
     for part in range(2):
         at = own[part] // CHUNK
-        keys, values = load(at)
+        keys, values = load_keys(at), load_values(at)
         for h in range(2):
             s = dot(q_buf[part, h], keys, NT)
             ki = lax.broadcasted_iota(jnp.int32, s.shape, 1) + (at * CHUNK - own[part]) * BLOCK
@@ -624,19 +651,33 @@
             p = jnp.exp2(s - new).astype(jnp.bfloat16)
             acc_buf[part, h] = dot(p, values, NN)
 
+    def place_of(i):
+        i = jnp.minimum(i, steps - 1)
+        part = (i >= wholes).astype(jnp.int32)
+        return part, i - part * wholes
+
+    def score(i, h):
+        part, at = place_of(i)
+        return dot(q_buf[part, h], load_keys(at), NT)
+
+    s_buf[...] = score(0, 0)
+
     def step(j, unused):
+        ready = s_buf[...]
         for n in range(unroll):
             i = j * unroll + n
-            part = (i >= wholes).astype(jnp.int32)
-            keys, values = load(i - part * wholes)
+            part, at = place_of(i)
+            values = load_values(at)
             for h in range(2):
-                s = dot(q_buf[part, h], keys, NT)
+                s = ready
+                ready = score(i + h, 1 - h)
                 old = m_buf[part, h]
                 new = jnp.maximum(old, jnp.max(s, axis=1, keepdims=True))
                 m_buf[part, h] = new
                 factor = jnp.exp2(old - new)
                 p = jnp.exp2(s - new[:, :1]).astype(jnp.bfloat16)
                 acc_buf[part, h] = acc_buf[part, h] * factor[:, :1] + dot(p, values, NN)
+        s_buf[...] = ready
         return unused
 
     lax.fori_loop(0, steps // unroll, step, 0)
@@ -647,13 +688,15 @@
                 acc[:, :HD] / acc[:, HD:]
             ).astype(jnp.bfloat16)
 
+    odd = (group // 2) % 2 == 1
     for h in range(2):
         base = stat_ref[:, h, :]
         best = jnp.max(base, axis=0, keepdims=True)
         share = stat_ref[:, 2 + h, :] * jnp.exp2(base - best)
         share = jnp.concatenate(
             [share, jnp.zeros((HD - chips, HD), jnp.float32)], axis=0
-        ).T[:fresh]
+        ).T
+        share = jnp.where(odd, share[HD // 2:HD // 2 + fresh], share[:fresh])
         numer = jnp.zeros((fresh, HD), jnp.float32)
         for g in range(chips):
             numer = numer + share[:, g:g + 1] * part_ref[g, :, h * HD:(h + 1) * HD].astype(
@@ -676,6 +719,7 @@
         out_specs=[vmem, vmem],
         scratch_shapes=[
             pltpu.VMEM((2, 2, BLOCK, 2 * HD), jnp.bfloat16),
+            pltpu.VMEM((BLOCK, CHUNK * BLOCK), jnp.float32),
             pltpu.VMEM((2, 2, BLOCK, HD), jnp.float32),
             pltpu.VMEM((2, 2, BLOCK, 2 * HD), jnp.float32),
             pltpu.SMEM((total,), jnp.int32),

time: 83.5 us -> 80.6 us (0.965)
  the two profiles are of different devices: /device:TPU:1 before, /device:TPU:33 now
where the time goes in v3:
time: 80.6 us; the launch traced here: 80.5 us
  Pallas kernels  79.9 us (99%)
    pallas_call x1, Pallas kernels, exchange(): pl.pallas_call(functools.partial(exchange_kernel, blocks, heads), out_sha...  64 us
    pallas_call x1, Pallas kernels, attend_a(): pl.pallas_call(functools.partial(a_kernel, fresh), out_shape=(jax.ShapeDt...  15.8 us

profile of v3, /device:TPU:33, one launch (start us, length us, event | category | flops | bytes accessed | tf_op | source)
XLA Modules:
  0.0 80.5 jit_solution(5087569661485164793)
XLA Ops:
  0.6 0.0 copy-start
  0.6 64.0 %exchange.1 = (bf16[2,8,2,4,2,64,128]{6,5,4,3,2,1,0:T(8,128)(2,1)S(1)}, bf16[2,8,2,4,2,64,128]{6,5,4,3,2,1,0:T(8,128)(2,1)S(1)}, bf16[16,48,256]{2,1,0:T(8,128)(...) custom-call(s32[32]{0:T(128)} %lengths_hbm.1, s32[16384]{0:T(1024)} %positions_hbm.1, bf16[64,128]{1,0:T(8,128)(2,1)} %a_key.1, ...), custom_call_target="tpu_custom_call" | custom-call | flops 10000000000 | bytes 20000000 | tf_op jit(solution)/shard_map/exchange/pallas_call | solution.py:554
  64.7 0.0 copy-done
  64.7 15.8 %attend_a.1 = (bf16[512,256]{1,0:T(8,128)(2,1)}, bf16[48,256]{1,0:T(8,128)(2,1)}) custom-call(s32[64]{0:T(128)S(1)} %get-tuple-element.7.pos_ref, bf16[512,256]{1,0:T(8,128)(2,1)S(1)} %copy-done, bf16[64,256,128]{2,1,0:T(8,128)(2,1)S(1)} %bitcast.2, bf16[64,256,128]{2,1,0:T(8,128)(2,1)S(1)} %bitcast.3, bf16[16,48,256]{2,1,0:T(8,128)(2,1)S(1)} %get-tuple-element.10.part_ref, ...), custom_call_target="tpu_custom_call" | custom-call | flops 10000000000 | bytes 9000000 | tf_op jit(solution)/shard_map/attend_a/pallas_call | solution.py:712
Async XLA Ops:
  0.6 64.1 %copy-start = (bf16[512,256]{1,0:T(8,128)(2,1)S(1)}, bf16[512,256]{1,0:T(8,128)(2,1)}, u32[]{:S(2)}) copy-start(bf16[512,256]{1,0:T(8,128)(2,1)} %q_ref.1) | copy-start | bytes 786436

commit v4 on v3

--- a/solution.py
+++ b/solution.py
@@ -220,8 +220,8 @@
     near = Gather(book, near_views, ["x"], axes, None)
     far = Gather(book, far_views, ["yh", "x"], axes, None)
     asked = Gather(book, query_views, ["yl", "z"], axes, sibling)
-    piece_x = Gather(book, a_views([(key_all, upper)], 0), ["z*", "y", "x"], axes, sibling)
-    piece_y = Gather(book, a_views([(value_all, upper)], 1), ["z*", "x", "y"], axes, sibling)
+    piece_x = Gather(book, a_views([(key_all, upper)], 0), ["z*", "y*", "x"], axes, sibling)
+    piece_y = Gather(book, a_views([(value_all, upper)], 1), ["z*", "x*", "y"], axes, sibling)
     piece_z = Gather(
         book, a_views([(key_all, lower), (value_all, lower)], 0), ["x*", "y*", "z"], axes, sibling
     )
@@ -265,24 +265,26 @@
     for copy in locals_[:-1]:
         copy.wait()
 
-    far.run(0)
-    near.run(0)
     asked.run(0)
-    piece_z.run(0)
     piece_x.run(0)
     piece_y.run(0)
+    near.run(0)
+    piece_z.run(0)
+    far.run(0)
     column[...] = jnp.zeros(column.shape, jnp.float32)
     k_buf[count + fresh:, :] = jnp.zeros((HD - fresh, HD), jnp.bfloat16)
     v_buf[count + fresh:, :HD] = jnp.zeros((HD - fresh, HD), jnp.bfloat16)
     v_buf[count:, HD:] = jnp.ones((HD, HD), jnp.bfloat16)
     asked.run(1)
-    piece_z.run(1)
     piece_x.run(1)
     piece_y.run(1)
+    piece_z.run(1)
     near.run(1)
     asked.run(2)
     piece_z.run(2)
     far.run(1)
+    piece_x.run(2)
+    piece_y.run(2)
     near.run(2)
     slots = k_all.shape[2]
     side = X * slots
@@ -306,23 +308,21 @@
     tile_rows = OWNERS * fresh
     soon = [
         (0, lambda: asked.run(3)),
-        (0, lambda: piece_x.run(2)),
-        (0, lambda: piece_y.run(2)),
         (1, lambda: asked.run(4)),
         (1, lambda: piece_z.run(3)),
         (2, lambda: asked.siblings(3, 5)),
         (2, lambda: far.run(2)),
         (3, lambda: asked.run(5)),
-        (3, lambda: piece_x.run(3)),
-        (3, lambda: piece_y.run(3)),
         (4, lambda: piece_z.run(4)),
         (6, lambda: asked.siblings(5)),
     ]
     late = [
+        (0, lambda: piece_x.run(3)),
+        (0, lambda: piece_y.run(3)),
         (0, lambda: piece_z.run(5)),
         (3, lambda: piece_z.run(6)),
-        (4, lambda: piece_x.run(4)),
-        (4, lambda: piece_y.run(4)),
+        (6, lambda: piece_x.run(4)),
+        (6, lambda: piece_y.run(4)),
     ]
 
     def serve(i, todo):
@@ -505,8 +505,6 @@
 
     lax.fori_loop(0, tiles, tile_step, 0)
     finish(tiles - 1)
-    piece_x.run(5)
-    piece_y.run(5)
     for copy in own_copies(0):
         copy.wait()
 
@@ -614,7 +612,7 @@
     own = [pos_ref[2 * group], pos_ref[2 * group + 1]]
     wholes = own[0] // CHUNK
     steps = total // CHUNK - 1
-    unroll = 3 if steps % 3 == 0 else 1
+    unroll = 5 if steps % 5 == 0 else 1
 
     def invert(i, unused):
         place[pos_ref[i]] = i

time: 80.6 us -> 80.9 us (level)
    pallas_call x1, Pallas kernels: 15.8 us -> 14.8 us  [attend_a(): pl.pallas_call(functools.partial(a_kernel, fresh), out_shape=(jax.ShapeDt...]
where the time goes in v4:
time: 80.9 us; the launch traced here: 80.1 us
  Pallas kernels  79.5 us (98%)
    pallas_call x1, Pallas kernels, exchange(): pl.pallas_call(functools.partial(exchange_kernel, blocks, heads), out_sha...  64.7 us
    pallas_call x1, Pallas kernels, attend_a(): pl.pallas_call(functools.partial(a_kernel, fresh), out_shape=(jax.ShapeDt...  14.8 us

profile of v4, /device:TPU:33, one launch (start us, length us, event | category | flops | bytes accessed | tf_op | source)
XLA Modules:
  0.0 80.1 jit_solution(2923507154371242721)
XLA Ops:
  0.6 0.0 copy-start
  0.6 64.7 %exchange.1 = (bf16[2,8,2,4,2,64,128]{6,5,4,3,2,1,0:T(8,128)(2,1)S(1)}, bf16[2,8,2,4,2,64,128]{6,5,4,3,2,1,0:T(8,128)(2,1)S(1)}, bf16[16,48,256]{2,1,0:T(8,128)(...) custom-call(s32[32]{0:T(128)} %lengths_hbm.1, s32[16384]{0:T(1024)} %positions_hbm.1, bf16[64,128]{1,0:T(8,128)(2,1)} %a_key.1, ...), custom_call_target="tpu_custom_call" | custom-call | flops 10000000000 | bytes 20000000 | tf_op jit(solution)/shard_map/exchange/pallas_call | solution.py:552
  65.3 0.0 copy-done
  65.3 14.8 %attend_a.1 = (bf16[512,256]{1,0:T(8,128)(2,1)}, bf16[48,256]{1,0:T(8,128)(2,1)}) custom-call(s32[64]{0:T(128)S(1)} %get-tuple-element.7.pos_ref, bf16[512,256]{1,0:T(8,128)(2,1)S(1)} %copy-done, bf16[64,256,128]{2,1,0:T(8,128)(2,1)S(1)} %bitcast.2, bf16[64,256,128]{2,1,0:T(8,128)(2,1)S(1)} %bitcast.3, bf16[16,48,256]{2,1,0:T(8,128)(2,1)S(1)} %get-tuple-element.10.part_ref, ...), custom_call_target="tpu_custom_call" | custom-call | flops 10000000000 | bytes 9000000 | tf_op jit(solution)/shard_map/attend_a/pallas_call | solution.py:710
Async XLA Ops:
  0.6 64.7 %copy-start = (bf16[512,256]{1,0:T(8,128)(2,1)S(1)}, bf16[512,256]{1,0:T(8,128)(2,1)}, u32[]{:S(2)}) copy-start(bf16[512,256]{1,0:T(8,128)(2,1)} %q_ref.1) | copy-start | bytes 786436

commit v5 on v3

--- a/solution.py
+++ b/solution.py
@@ -11,7 +11,7 @@
 HD = 128
 BLOCK = 256
 CHUNK = 4
-OWNERS = 4
+OWNERS = 8
 SCALE2 = HD ** (-0.5) * math.log2(math.e)
 LOWEST = -1e30
 NT = (((1,), (1,)), ((), ()))
@@ -302,7 +302,7 @@
     asked.siblings(0, 3)
 
     tiles = blocks // OWNERS
-    zs_tile = OWNERS // 2
+    mine_tile = OWNERS // 2
     tile_rows = OWNERS * fresh
     soon = [
         (0, lambda: asked.run(3)),
@@ -310,35 +310,39 @@
         (0, lambda: piece_y.run(2)),
         (1, lambda: asked.run(4)),
         (1, lambda: piece_z.run(3)),
-        (2, lambda: asked.siblings(3, 5)),
-        (2, lambda: far.run(2)),
-        (3, lambda: asked.run(5)),
-        (3, lambda: piece_x.run(3)),
-        (3, lambda: piece_y.run(3)),
-        (4, lambda: piece_z.run(4)),
-        (6, lambda: asked.siblings(5)),
+        (1, lambda: far.run(2)),
+        (1, lambda: asked.siblings(3, 5)),
+        (2, lambda: piece_x.run(3)),
+        (2, lambda: piece_y.run(3)),
+        (2, lambda: asked.run(5)),
+        (3, lambda: piece_z.run(4)),
+        (3, lambda: asked.siblings(5)),
     ]
     late = [
         (0, lambda: piece_z.run(5)),
-        (3, lambda: piece_z.run(6)),
-        (4, lambda: piece_x.run(4)),
-        (4, lambda: piece_y.run(4)),
+        (2, lambda: piece_z.run(6)),
+        (2, lambda: piece_x.run(4)),
+        (2, lambda: piece_y.run(4)),
     ]
 
     def serve(i, todo):
-        for at in range(tiles):
-            now = [act for when, act in todo if min(when, tiles - 1) == at]
-            if now:
-                @pl.when(i == at)
-                def _():
-                    for act in now:
-                        act()
+        for when, act in todo:
+            if min(when, tiles - 1) == i:
+                act()
 
     def tile_of(i):
-        pairs, k = Z // 2, i // 2
-        away = ((k + 1) // 2) * (2 * (k % 2) - 1)
-        yl_at, z_at = (yl + i) % 2, ((z // 2 + away + pairs) % pairs) * 2
-        return yl_at * (2 * Z) + 2 * z_at, yl_at, z_at
+        pairs = Z // 2
+        away = ((i + 1) // 2) * (2 * (i % 2) - 1)
+        return ((z // 2 + away + pairs) % pairs) * 2
+
+    def queries_of(i):
+        return jnp.concatenate(
+            [
+                q_all[yl_at, pl.ds(tile_of(i), 2)].reshape(tile_rows // 2, 2 * HD)
+                for yl_at in range(YL)
+            ],
+            axis=0,
+        )
 
     def near_copies(i):
         return [
@@ -364,7 +368,7 @@
                 device_id_type=MESH,
             )
             for n, (a, b) in enumerate(
-                ((part_out.at[source], part_in), (stat_out.at[source // zs_tile], stat_in))
+                ((part_out.at[source], part_in), (stat_out.at[source // 2], stat_in))
             )
         ]
 
@@ -372,49 +376,60 @@
         return [
             pltpu.make_async_copy(a, b.at[mine], local.at[n])
             for n, (a, b) in enumerate(
-                ((part_out.at[source], part_in), (stat_out.at[source // zs_tile], stat_in))
+                ((part_out.at[source], part_in), (stat_out.at[source // 2], stat_in))
             )
         ]
 
-    lane = lax.broadcasted_iota(jnp.int32, (fresh, HD), 1)
-
-    def finish(i):
-        for copy in near_copies(i):
-            copy.wait_recv()
-        first, yl_at, z_at = tile_of(i)
-        for n in range(zs_tile):
-            ours, theirs = col[i, c, n], col_near[i, n]
-            stats = []
+    half_rows = mine_tile * fresh
+    lane = lax.broadcasted_iota(jnp.int32, (half_rows, HD), 1)
+
+    def weigh(i):
+        ours = col[i, c].reshape(half_rows, HD)
+        theirs = col_near[i].reshape(half_rows, HD)
+        stats, merged = [], []
+        for h in range(2):
+            base0, base1 = ours[:, h:h + 1], theirs[:, h:h + 1]
+            base = jnp.maximum(base0, base1)
+            share0 = ours[:, 2 + h:3 + h] * jnp.exp2(base0 - base)
+            share1 = theirs[:, 2 + h:3 + h] * jnp.exp2(base1 - base)
+            total = share0 + share1
+            at = slice(h * HD, (h + 1) * HD)
+            both = share0 * part[i, c, :, :, at].reshape(half_rows, HD).astype(
+                jnp.float32
+            ) + share1 * part_near[i, :, :, at].reshape(half_rows, HD).astype(jnp.float32)
+            merged.append((both / total).astype(jnp.bfloat16))
+            stats += [base, total]
+        packed = jnp.where(
+            lane == 0,
+            stats[0],
+            jnp.where(lane == 1, stats[2], jnp.where(lane == 2, stats[1], stats[3])),
+        )
+        for j in range(mine_tile):
+            rows_j = slice(j * fresh, (j + 1) * fresh)
             for h in range(2):
-                base0, base1 = ours[:, h:h + 1], theirs[:, h:h + 1]
-                base = jnp.maximum(base0, base1)
-                share0 = ours[:, 2 + h:3 + h] * jnp.exp2(base0 - base)
-                share1 = theirs[:, 2 + h:3 + h] * jnp.exp2(base1 - base)
-                total = share0 + share1
-                at = slice(h * HD, (h + 1) * HD)
-                both = share0 * part[i, c, n, :, at].astype(jnp.float32) + share1 * part_near[
-                    i, n, :, at
-                ].astype(jnp.float32)
-                part_out[zs_tile * i + n, :, at] = (both / total).astype(jnp.bfloat16)
-                stats += [base, total]
-            column[n * (HD // 2):n * (HD // 2) + fresh, :] = jnp.where(
-                lane == 0,
-                stats[0],
-                jnp.where(lane == 1, stats[2], jnp.where(lane == 2, stats[1], stats[3])),
-            )
-        stat_out[i] = column[...].T[:8]
-        for n in range(zs_tile):
-            owner = first + 2 * n + c
-            slot = yl_at * Z + z_at + n
-
-            @pl.when(owner != me)
-            def _():
-                for copy in merge_copies(zs_tile * i + n, mine, owner, slot):
+                part_out[mine_tile * i + j, :, h * HD:(h + 1) * HD] = merged[h][rows_j]
+            column[j * (HD // 2):j * (HD // 2) + fresh, :] = packed[rows_j]
+        for n in range(YL):
+            stat_out[YL * i + n] = column[n * HD:(n + 1) * HD, :].T[:8]
+
+    def deliver(i):
+        for j in range(mine_tile):
+            slot = (j // 2) * Z + tile_of(i) + j % 2
+            owner = 2 * slot + c
+
+            def away():
+                for copy in merge_copies(mine_tile * i + j, mine, owner, slot):
                     copy.start()
+
+            if i > 0:
+                away()
+                continue
+
+            pl.when(owner != me)(away)
 
             @pl.when(owner == me)
             def _():
-                for copy in own_copies(zs_tile * i + n):
+                for copy in own_copies(j):
                     copy.start()
 
     wide = lax.broadcasted_iota(jnp.int32, (tile_rows, HD), 1)
@@ -424,11 +439,10 @@
             wide == 0, bases[0], jnp.where(wide == 1, bases[1], jnp.where(wide == 2, sums[0], sums[1]))
         )
 
-    def near_step(i, unused):
+    def near_step(i):
         serve(i, soon)
 
-        first, yl_at, z_at = tile_of(i)
-        q = q_all[yl_at, pl.ds(z_at, zs_tile)].reshape(tile_rows, 2 * HD)
+        q = queries_of(i)
         bases, sums = [], []
         both = [dot(q[:, h * HD:(h + 1) * HD], k_buf[:side, :], NT) for h in range(2)]
         for h, scores in enumerate(both):
@@ -439,9 +453,9 @@
             bases.append(jnp.where(yh * slots < limit, base, LOWEST))
             sums.append(acc[:, HD:HD + 1])
         held_col[i] = pack(bases, sums)
-        return unused
-
-    lax.fori_loop(0, tiles, near_step, 0)
+
+    for i in range(tiles):
+        near_step(i)
     far.run(3)
     locals_[-1].wait()
 
@@ -452,11 +466,13 @@
     lax.fori_loop(0, order.shape[0], label, 0)
     prepare(1 - yh, k_all[0, 0][:1].astype(jnp.float32))
 
-    def tile_step(i, unused):
+    def tile_step(i):
         serve(i, late)
-
-        first, yl_at, z_at = tile_of(i)
-        q = q_all[yl_at, pl.ds(z_at, zs_tile)].reshape(tile_rows, 2 * HD)
+        if i > 0:
+            for copy in near_copies(i - 1):
+                copy.wait_recv()
+
+        q = queries_of(i)
         before = held_col[i]
         bases, sums, outs = [], [], []
         both = [
@@ -468,7 +484,10 @@
         ]
         for h, (scores, extra) in enumerate(both):
             ki = lax.broadcasted_iota(jnp.int32, extra.shape, 1)
-            ti = lax.broadcasted_iota(jnp.int32, extra.shape, 0) + first * fresh
+            ti = lax.broadcasted_iota(jnp.int32, extra.shape, 0)
+            ti = ti + 2 * tile_of(i) * fresh + jnp.where(
+                ti >= half_rows, 2 * Z * fresh - half_rows, 0
+            )
             seen = jnp.logical_and(ki < fresh, ki + me * fresh <= ti)
             extra = jnp.where(seen, extra, LOWEST)
             top = jnp.maximum(
@@ -494,17 +513,19 @@
             for h in range(2):
                 part[i, j % 2, j // 2, :, h * HD:(h + 1) * HD] = outs[h][at]
             col[i, j % 2, j // 2] = packed[at]
+        if i > 0:
+            weigh(i - 1)
         for copy in near_copies(i):
             copy.start()
-
-        @pl.when(i > 0)
-        def _():
-            finish(i - 1)
-
-        return unused
-
-    lax.fori_loop(0, tiles, tile_step, 0)
-    finish(tiles - 1)
+        if i > 0:
+            deliver(i - 1)
+
+    for i in range(tiles):
+        tile_step(i)
+    for copy in near_copies(tiles - 1):
+        copy.wait_recv()
+    weigh(tiles - 1)
+    deliver(tiles - 1)
     piece_x.run(5)
     piece_y.run(5)
     for copy in own_copies(0):
@@ -576,9 +597,9 @@
             pltpu.VMEM((tiles, half, fresh, HD), jnp.float32),
             pltpu.VMEM((tiles, OWNERS * fresh, 2 * HD), jnp.float32),
             pltpu.VMEM((tiles, OWNERS * fresh, HD), jnp.float32),
-            pltpu.VMEM((HD, HD), jnp.float32),
+            pltpu.VMEM((2 * HD, HD), jnp.float32),
             pltpu.VMEM((chips, fresh, 2 * HD), jnp.bfloat16),
-            pltpu.VMEM((tiles, 8, HD), jnp.float32),
+            pltpu.VMEM((YL * tiles, 8, HD), jnp.float32),
             pltpu.SemaphoreType.DMA((copies,)),
             pltpu.SemaphoreType.DMA((copies,)),
             pltpu.SemaphoreType.DMA((2, tiles)),
@@ -614,7 +635,7 @@
     own = [pos_ref[2 * group], pos_ref[2 * group + 1]]
     wholes = own[0] // CHUNK
     steps = total // CHUNK - 1
-    unroll = 3 if steps % 3 == 0 else 1
+    unroll = 5 if steps % 5 == 0 else 1
 
     def invert(i, unused):
         place[pos_ref[i]] = i

time: 80.6 us -> 80.9 us (level); the launches traced: 80.5 us -> 80 us
    pallas_call x1, Pallas kernels: 15.8 us -> 14.8 us  [attend_a(): pl.pallas_call(functools.partial(a_kernel, fresh), out_shape=(jax.ShapeDt...]
where the time goes in v5:
time: 80.9 us; the launch traced here: 80 us
  Pallas kernels  79.3 us (98%)
    pallas_call x1, Pallas kernels, exchange(): pl.pallas_call(functools.partial(exchange_kernel, blocks, heads), out_sha...  64.5 us
    pallas_call x1, Pallas kernels, attend_a(): pl.pallas_call(functools.partial(a_kernel, fresh), out_shape=(jax.ShapeDt...  14.8 us

profile of v5, /device:TPU:33, one launch (start us, length us, event | category | flops | bytes accessed | tf_op | source)
XLA Modules:
  0.0 80.0 jit_solution(5864709449670606410)
XLA Ops:
  0.6 0.0 copy-start
  0.6 64.5 %exchange.1 = (bf16[2,8,2,4,2,64,128]{6,5,4,3,2,1,0:T(8,128)(2,1)S(1)}, bf16[2,8,2,4,2,64,128]{6,5,4,3,2,1,0:T(8,128)(2,1)S(1)}, bf16[16,48,256]{2,1,0:T(8,128)(...) custom-call(s32[32]{0:T(128)} %lengths_hbm.1, s32[16384]{0:T(1024)} %positions_hbm.1, bf16[64,128]{1,0:T(8,128)(2,1)} %a_key.1, ...), custom_call_target="tpu_custom_call" | custom-call | flops 10000000000 | bytes 20000000 | tf_op jit(solution)/shard_map/exchange/pallas_call | solution.py:575
  65.1 0.0 copy-done
  65.2 14.8 %attend_a.1 = (bf16[512,256]{1,0:T(8,128)(2,1)}, bf16[48,256]{1,0:T(8,128)(2,1)}) custom-call(s32[64]{0:T(128)S(1)} %get-tuple-element.7.pos_ref, bf16[512,256]{1,0:T(8,128)(2,1)S(1)} %copy-done, bf16[64,256,128]{2,1,0:T(8,128)(2,1)S(1)} %bitcast.2, bf16[64,256,128]{2,1,0:T(8,128)(2,1)S(1)} %bitcast.3, bf16[16,48,256]{2,1,0:T(8,128)(2,1)S(1)} %get-tuple-element.10.part_ref, ...), custom_call_target="tpu_custom_call" | custom-call | flops 10000000000 | bytes 9000000 | tf_op jit(solution)/shard_map/attend_a/pallas_call | solution.py:733
Async XLA Ops:
  0.6 64.5 %copy-start = (bf16[512,256]{1,0:T(8,128)(2,1)S(1)}, bf16[512,256]{1,0:T(8,128)(2,1)}, u32[]{:S(2)}) copy-start(bf16[512,256]{1,0:T(8,128)(2,1)} %q_ref.1) | copy-start | bytes 786436

commit v6 on v5

--- a/solution.py
+++ b/solution.py
@@ -309,18 +309,18 @@
         (0, lambda: piece_x.run(2)),
         (0, lambda: piece_y.run(2)),
         (1, lambda: asked.run(4)),
+        (1, lambda: far.run(2)),
+        (1, lambda: piece_x.run(3)),
+        (1, lambda: piece_y.run(3)),
         (1, lambda: piece_z.run(3)),
-        (1, lambda: far.run(2)),
         (1, lambda: asked.siblings(3, 5)),
-        (2, lambda: piece_x.run(3)),
-        (2, lambda: piece_y.run(3)),
         (2, lambda: asked.run(5)),
-        (3, lambda: piece_z.run(4)),
+        (2, lambda: piece_z.run(4)),
+        (3, lambda: piece_z.run(5)),
         (3, lambda: asked.siblings(5)),
     ]
     late = [
-        (0, lambda: piece_z.run(5)),
-        (2, lambda: piece_z.run(6)),
+        (0, lambda: piece_z.run(6)),
         (2, lambda: piece_x.run(4)),
         (2, lambda: piece_y.run(4)),
     ]

time: 80.9 us -> 86.1 us (1.064)
  Pallas kernels: 79.3 us -> 85.3 us
    pallas_call x1, Pallas kernels: 64.5 us -> 70.4 us  [exchange(): pl.pallas_call(functools.partial(exchange_kernel, blocks, heads), out_sha...]
where the time goes in v6:
time: 86.1 us; the launch traced here: 85.9 us
  Pallas kernels  85.3 us (99%)
    pallas_call x1, Pallas kernels, exchange(): pl.pallas_call(functools.partial(exchange_kernel, blocks, heads), out_sha...  70.4 us
    pallas_call x1, Pallas kernels, attend_a(): pl.pallas_call(functools.partial(a_kernel, fresh), out_shape=(jax.ShapeDt...  14.8 us

profile of v6, /device:TPU:33, one launch (start us, length us, event | category | flops | bytes accessed | tf_op | source)
XLA Modules:
  0.0 85.9 jit_solution(2451218820005712863)
XLA Ops:
  0.6 0.0 copy-start
  0.6 70.4 %exchange.1 = (bf16[2,8,2,4,2,64,128]{6,5,4,3,2,1,0:T(8,128)(2,1)S(1)}, bf16[2,8,2,4,2,64,128]{6,5,4,3,2,1,0:T(8,128)(2,1)S(1)}, bf16[16,48,256]{2,1,0:T(8,128)(...) custom-call(s32[32]{0:T(128)} %lengths_hbm.1, s32[16384]{0:T(1024)} %positions_hbm.1, bf16[64,128]{1,0:T(8,128)(2,1)} %a_key.1, ...), custom_call_target="tpu_custom_call" | custom-call | flops 10000000000 | bytes 20000000 | tf_op jit(solution)/shard_map/exchange/pallas_call | solution.py:575
  71.1 0.0 copy-done
  71.1 14.8 %attend_a.1 = (bf16[512,256]{1,0:T(8,128)(2,1)}, bf16[48,256]{1,0:T(8,128)(2,1)}) custom-call(s32[64]{0:T(128)S(1)} %get-tuple-element.7.pos_ref, bf16[512,256]{1,0:T(8,128)(2,1)S(1)} %copy-done, bf16[64,256,128]{2,1,0:T(8,128)(2,1)S(1)} %bitcast.2, bf16[64,256,128]{2,1,0:T(8,128)(2,1)S(1)} %bitcast.3, bf16[16,48,256]{2,1,0:T(8,128)(2,1)S(1)} %get-tuple-element.10.part_ref, ...), custom_call_target="tpu_custom_call" | custom-call | flops 10000000000 | bytes 9000000 | tf_op jit(solution)/shard_map/attend_a/pallas_call | solution.py:733
Async XLA Ops:
  0.6 70.5 %copy-start = (bf16[512,256]{1,0:T(8,128)(2,1)S(1)}, bf16[512,256]{1,0:T(8,128)(2,1)}, u32[]{:S(2)}) copy-start(bf16[512,256]{1,0:T(8,128)(2,1)} %q_ref.1) | copy-start | bytes 786436
